TPU v7x, 256 devices: a whole 4x4x8 slice. The times are simulated.
256 devices in a mesh: seq: 32 (over z_hi, x, core), head: 8 (over z_lo, y).
Axes of the slice: x: 4, y: 4, z: 8 (z_hi: 4, z_lo: 2; z = z_hi * 2 + z_lo), core: 2. Of those that a mesh axis runs over, the one named last changes fastest.
Arguments:
- query: bfloat16 [16384, 5120], P(('seq', 'head')), may hold values from -15 to 15
- key_in: bfloat16 [16384, 5120], P(('seq', 'head')), may hold values from -15 to 15
- value: bfloat16 [16384, 5120], P(('seq', 'head')), may hold values from -6 to 6
- query_gain: float32 [5120], replicated, may hold values from 0.1 to 1.9
- key_gain: float32 [5120], replicated, may hold values from 0.1 to 1.9
- tile_lists: int32 [128, 20], replicated, may hold values from 0 to 127, as said below
- list_lengths: int32 [128], replicated, may hold values from 12 to 20
Outputs:
- attended: bfloat16 [16384, 5120], P(('seq', 'head'))
Inputs may be any that keep to these rules, and one draw needn't show every extreme that they name: `tile_lists`: entries of row t past list_lengths[t] are 0. The first 4 entries of row t are the tiles g*4 to g*4 + 3 in order, g = t // 4; the further valid entries are distinct tiles outside that group. Over the 4 query tiles of one group, exactly 1 distinct tiles of every other group are listed.
All inputs are finite; a program needn't handle non-finite values.
Results may differ from a plain program's by a relative error of at most 0.012.
The roundings to bfloat16 on the way count: a program that leaves them out, or rounds other values in their place, can miss the bound.
Values may be sent and summed in bfloat16 or wider, within the bound.
A program may use at most 128 MiB of HBM per device.

v0:
```python
import jax
import jax.numpy as jnp
from jax import lax
from jax.sharding import PartitionSpec as P

HD = 128
TILE = 128
CAP = 1


def normalize(rows, gain):
    values = rows.astype(jnp.float32)
    square_mean = jnp.mean(values * values, axis=1, keepdims=True)
    return (values * lax.rsqrt(square_mean + 1e-06) * gain).astype(jnp.bfloat16)


def online_update(running, q_tile, key_block, value_block, is_valid):
    run_max, run_total, run_acc = running
    scores = jnp.einsum(
        "qhd,khd->hqk", q_tile, key_block, preferred_element_type=jnp.float32
    ) * HD ** (-0.5)
    scores = jnp.where(is_valid[None, None, :], scores, -1e30)
    new_max = jnp.maximum(run_max, jnp.max(scores, axis=-1))
    shrink = jnp.exp(run_max - new_max)
    raw = jnp.where(is_valid[None, None, :], jnp.exp(scores - new_max[:, :, None]), 0.0)
    weights = raw.astype(jnp.bfloat16)
    new_total = run_total * shrink + jnp.sum(raw, axis=-1)
    mixed = jnp.einsum("hqk,khd->qhd", weights, value_block, preferred_element_type=jnp.float32)
    new_acc = run_acc * jnp.transpose(shrink)[:, :, None] + mixed
    return (new_max, new_total, new_acc)


def finish(running):
    run_max, run_total, run_acc = running
    return (run_acc / jnp.transpose(run_total)[:, :, None]).astype(jnp.bfloat16)


def pad_columns(index_rows):
    extra = -index_rows.shape[1] % 4
    return index_rows


def run_entries(running, q_tile, kv_source, index_row, entry_count):
    block_tiles = 4
    block_count = (entry_count + block_tiles - 1) // block_tiles
    tile_rows = kv_source.shape[2]

    def advance(block_no, state):
        picked = lax.dynamic_slice_in_dim(index_row, block_no * block_tiles, block_tiles)
        chosen = jnp.take(kv_source, picked, axis=0)
        key_block = chosen[:, 0].reshape(block_tiles * tile_rows, chosen.shape[3], chosen.shape[4])
        value_block = chosen[:, 1].reshape(
            block_tiles * tile_rows, chosen.shape[3], chosen.shape[4]
        )
        is_valid = jnp.repeat(
            block_no * block_tiles + jnp.arange(block_tiles) < entry_count, tile_rows
        )
        return online_update(state, q_tile, key_block, value_block, is_valid)

    return lax.fori_loop(0, block_count, advance, running)


def fetch_tiles(key_heads, value_heads, tile_lists, list_lengths, group_total, my_group):
    group_rows, feat_width = key_heads.shape
    tiles_here = group_rows // TILE
    tile_total, list_width = tile_lists.shape
    entry_ok = jnp.arange(list_width)[None, :] < list_lengths[:, None]
    asker = jnp.arange(tile_total) // tiles_here
    entry_ok = entry_ok & (asker != my_group)[:, None]
    mine = my_group * tiles_here + jnp.arange(tiles_here)
    wanted = (tile_lists[:, :, None] == mine[None, None, :]) & entry_ok[:, :, None]
    needed = jnp.any(wanted, axis=1).reshape(group_total, tiles_here, tiles_here)
    needed = jnp.any(needed, axis=1).astype(jnp.int32)
    slot_rank = jnp.cumsum(needed, axis=1) - 1
    select = (needed[:, None, :] == 1) & (slot_rank[:, None, :] == jnp.arange(CAP)[None, :, None])
    select = select.astype(jnp.bfloat16).reshape(group_total * CAP, tiles_here)
    stacked = jnp.concatenate(
        [
            key_heads.reshape(tiles_here, TILE * feat_width),
            value_heads.reshape(tiles_here, TILE * feat_width),
        ],
        axis=1,
    )
    outgoing = jnp.dot(select, stacked, preferred_element_type=jnp.float32).astype(jnp.bfloat16)
    return lax.all_to_all(outgoing, "seq", split_axis=0, concat_axis=0, tiled=True)


def local(query, key_in, value, query_gain, key_gain, tile_lists, list_lengths):
    group_total = lax.axis_size("seq")
    my_group = lax.axis_index("seq")
    query_norm = normalize(query, query_gain)
    key_norm = normalize(key_in, key_gain)
    query_heads, key_heads, value_heads = (
        lax.all_to_all(query_norm, "head", split_axis=1, concat_axis=0, tiled=True),
        lax.all_to_all(key_norm, "head", split_axis=1, concat_axis=0, tiled=True),
        lax.all_to_all(value, "head", split_axis=1, concat_axis=0, tiled=True),
    )
    received = fetch_tiles(key_heads, value_heads, tile_lists, list_lengths, group_total, my_group)
    group_rows, feat_width = key_heads.shape
    tiles_here = group_rows // TILE
    head_count = feat_width // HD
    tile_total, list_width = tile_lists.shape
    own_lists = lax.dynamic_slice_in_dim(tile_lists, my_group * tiles_here, tiles_here, 0)
    own_lengths = lax.dynamic_slice_in_dim(list_lengths, my_group * tiles_here, tiles_here, 0)
    list_group = own_lists // tiles_here
    entry_ok = jnp.arange(list_width)[None, :] < own_lengths[:, None]
    remote_ok = entry_ok & (list_group != my_group)
    match = (own_lists[:, :, None] == jnp.arange(tile_total)[None, None, :]) & remote_ok[:, :, None]
    used_tiles = jnp.any(match, axis=(0, 1)).reshape(group_total, tiles_here).astype(jnp.int32)
    slot_rank = (jnp.cumsum(used_tiles, axis=1) - 1).reshape(tile_total)
    slot_entry = jnp.sum(jnp.where(match, slot_rank[None, None, :], 0), axis=2)
    remote_index = list_group * CAP + slot_entry
    q_tiles = query_heads.reshape(tiles_here, TILE, head_count, HD)
    far_pool = received.reshape(group_total * CAP, 2, TILE, head_count, HD)
    start_state = (
        jnp.full((head_count, TILE), -1e30, jnp.float32),
        jnp.zeros((head_count, TILE), jnp.float32),
        jnp.zeros((TILE, head_count, HD), jnp.float32),
    )
    near_pool = jnp.stack(
        [
            key_heads.reshape(tiles_here, TILE, head_count, HD),
            value_heads.reshape(tiles_here, TILE, head_count, HD),
        ],
        axis=1,
    )
    kv_pool = jnp.concatenate([near_pool, far_pool], axis=0)
    pool_index = jnp.where(
        list_group == my_group, own_lists % tiles_here, tiles_here + remote_index
    )

    def whole_tile(packed):
        q_tile, index_row, entry_count = packed
        return finish(run_entries(start_state, q_tile, kv_pool, index_row, entry_count))

    attended = lax.map(whole_tile, (q_tiles, pad_columns(pool_index), own_lengths))
    attended = attended.reshape(group_rows, feat_width)
    return lax.all_to_all(attended, "head", split_axis=0, concat_axis=1, tiled=True)


def solution(mesh):
    in_specs = (
        P(("seq", "head"), None),
        P(("seq", "head"), None),
        P(("seq", "head"), None),
        P(),
        P(),
        P(),
        P(),
    )
    out_specs = P(("seq", "head"), None)
    return jax.shard_map(local, mesh=mesh, in_specs=in_specs, out_specs=out_specs, check_vma=False)
```

profile of v0, /device:TPU:6, one launch (start us, length us, event | category | flops | bytes accessed | tf_op | source)
XLA Modules:
  0.0 680.6 jit_solution(14946464603488714015)
XLA Ops:
  10.7 9.5 %all-to-all-done.1 = bf16[64,8,640]{2,0,1:T(8,128)(2,1)S(1)} async-done(((bf16[64,8,640]{2,0,1:T(8,128)(2,1)}), bf16[64,8,640]{2,0,1:T(8,128)(2,1)S(1)}, u32[]{:S(2)}, u32[]{:S(2)}) %all-to-all-start.1) | async-done | bytes 655392 | tf_op jit(solution)/shard_map/all_to_all | solution.py:95
  24.9 9.7 %all-to-all-done.2 = bf16[64,8,640]{2,0,1:T(8,128)(2,1)S(1)} async-done(((bf16[64,8,640]{2,0,1:T(8,128)(2,1)}), bf16[64,8,640]{2,0,1:T(8,128)(2,1)S(1)}, u32[]{:S(2)}, u32[]{:S(2)}) %all-to-all-start.2) | async-done | bytes 655392 | tf_op jit(solution)/shard_map/all_to_all | solution.py:96
  39.1 10.4 %fusion.13 = bf16[32,1,163840]{2,0,1:T(8,128)(2,1)} fusion(bf16[4,81920]{1,0:T(4,128)(2,1)S(1)} %reshape.143, bf16[4,81920]{1,0:T(4,128)(2,1)S(1)} %reshape.142, s32[32,4]{0,1:T(4,128)S(1)} %reduce_window_sum.18, pred[32,4]{0,1:T(4,128)(4,1)S(1)} %reduce_or.29), kind=kOutput, calls=%fused_computation.29 | convolution fusion | flops 49808000 | bytes 11797120 | tf_op jit(solution)/shard_map/dot_general | solution.py:84
  50.2 13.3 %reduce.1 = bf16[32,163840]{1,0:T(8,128)(2,1)} reduce(bf16[32,1,163840]{2,0,1:T(8,128)(2,1)} %fusion.13, bf16[]{:T(256)} %broadcast.186), dimensions={1}, to_apply=%copy.75.reduce_sub_computation | reduce | bytes 20971522 | tf_op jit(solution)/shard_map/all_to_all | solution.py:85
  63.4 13.2 %reshape.156 = bf16[32,2,81920]{2,1,0:T(2,128)(2,1)} reshape(bf16[32,163840]{1,0:T(8,128)(2,1)} %reduce.1) | data formatting | bytes 20971520
  77.5 10.7 %all-to-all-start.3 = ((bf16[32,2,81920]{2,1,0:T(2,128)(2,1)}), bf16[32,2,81920]{2,1,0:T(2,128)(2,1)}, u32[]{:S(2)}, u32[]{:S(2)}) async-start(bf16[32,2,81920]{2,1,0:T(2,128)(2,1)} %reshape.156), calls=%async_computation.3 | async-start | bytes 20971520 | tf_op jit(solution)/shard_map/all_to_all | solution.py:85
  93.8 226.1 %all-to-all-done.3 = bf16[32,2,81920]{2,1,0:T(2,128)(2,1)} async-done(((bf16[32,2,81920]{2,1,0:T(2,128)(2,1)}), bf16[32,2,81920]{2,1,0:T(2,128)(2,1)}, u32[]{:S(2)}, u32[]{:S(2)}) %all-to-all-start.3) | async-done | bytes 10485792 | tf_op jit(solution)/shard_map/all_to_all | solution.py:85
  319.9 25.5 %reshape.157 = bf16[32,1,163840]{2,1,0:T(2,128)(2,1)} reshape(bf16[32,2,81920]{2,1,0:T(2,128)(2,1)} %all-to-all-done.3) | data formatting | bytes 20971520
  345.4 63.5 %reduce = bf16[32,163840]{1,0:T(8,128)(2,1)} reduce(bf16[32,1,163840]{2,1,0:T(2,128)(2,1)} %reshape.157, bf16[]{:T(256)} %constant.196), dimensions={1}, to_apply=%all_to_all.66.reduce_sub_computation | reduce | bytes 20971522 | tf_op jit(solution)/shard_map/all_to_all | solution.py:85
  408.9 19.3 %reshape.144 = bf16[32,2,128,5,128]{4,3,2,1,0:T(8,128)(2,1)} reshape(bf16[32,163840]{1,0:T(8,128)(2,1)} %reduce) | data formatting | bytes 20971520 | tf_op jit(solution)/shard_map/reshape | solution.py:114
  428.2 18.0 %pad_maximum_fusion = bf16[36,2,128,5,128]{4,3,2,1,0:T(8,128)(2,1)} fusion(bf16[32,2,128,5,128]{4,3,2,1,0:T(8,128)(2,1)} %reshape.144, bf16[4,1,128,5,128]{4,3,2,0,1:T(8,128)(2,1)S(1)} %stack_reshape.7, bf16[4,1,128,5,128]{4,3,2,0,1:T(8,128)(2,1)S(1)} %stack_reshape.6), kind=kLoop, calls=%fused_computation.30 | loop fusion | flops 24248320 | bytes 23592960 | tf_op jit(solution)/shard_map/concatenate | solution.py:127
  446.2 215.9 %while.58 = (s32[]{:T(128)}, bf16[4,128,5,128]{1,3,2,0:T(8,128)(2,1)}, s32[4]{0:T(128)S(1)}, s32[4,20]{1,0:T(4,128)S(1)}, bf16[4,128,5,128]{3,1,2,0:T(8,128)(2,1...) while((s32[]{:T(128)}, ...), condition=%wide.region_13.14_spmd, body=%wide.region_8.13_spmd.sunk | while | flops 171707312 | bytes 16440182 | solution.py:136
  448.4 51.0 %while.59 = (s32[]{:T(128)}, f32[5,128]{1,0:T(8,128)S(1)}, f32[5,128]{1,0:T(8,128)S(1)}, f32[128,5,128]{0,2,1:T(8,128)S(1)}, s32[]{:T(128)}, /*index=5*/s32[]{:T...) while((s32[]{:T(128)}, f32[5,128]{1,0:T(8,128)S(1)}, ...), condition=%wide.region_12.12_spmd, body=%wide.region_9.11_spmd.sunk | while | flops 171543456 | bytes 15284487 | solution.py:60
  449.1 7.3 %gather_fusion = bf16[4,2,128,5,128]{4,3,2,1,0:T(8,128)(2,1)S(1)} fusion(bf16[36,2,128,5,128]{4,3,2,1,0:T(8,128)(2,1)} %get-tuple-element.436, s32[1024]{0:T(1024)S(1)} %pad_clamp_fusion.2), kind=kCustom, calls=%fused_computation.clone.1 | custom fusion | bytes 2621456 | tf_op jit(solution)/shard_map/while/body/eval_jaxpr/while/body/jit(_take)/gather | solution.py:50
  459.3 7.3 %gather_fusion = bf16[4,2,128,5,128]{4,3,2,1,0:T(8,128)(2,1)S(1)} fusion(bf16[36,2,128,5,128]{4,3,2,1,0:T(8,128)(2,1)} %get-tuple-element.436, s32[1024]{0:T(1024)S(1)} %pad_clamp_fusion.2), kind=kCustom, calls=%fused_computation.clone.1 | custom fusion | bytes 2621456 | tf_op jit(solution)/shard_map/while/body/eval_jaxpr/while/body/jit(_take)/gather | solution.py:50
  469.5 7.3 %gather_fusion = bf16[4,2,128,5,128]{4,3,2,1,0:T(8,128)(2,1)S(1)} fusion(bf16[36,2,128,5,128]{4,3,2,1,0:T(8,128)(2,1)} %get-tuple-element.436, s32[1024]{0:T(1024)S(1)} %pad_clamp_fusion.2), kind=kCustom, calls=%fused_computation.clone.1 | custom fusion | bytes 2621456 | tf_op jit(solution)/shard_map/while/body/eval_jaxpr/while/body/jit(_take)/gather | solution.py:50
  479.7 7.3 %gather_fusion = bf16[4,2,128,5,128]{4,3,2,1,0:T(8,128)(2,1)S(1)} fusion(bf16[36,2,128,5,128]{4,3,2,1,0:T(8,128)(2,1)} %get-tuple-element.436, s32[1024]{0:T(1024)S(1)} %pad_clamp_fusion.2), kind=kCustom, calls=%fused_computation.clone.1 | custom fusion | bytes 2621456 | tf_op jit(solution)/shard_map/while/body/eval_jaxpr/while/body/jit(_take)/gather | solution.py:50
  489.9 7.3 %gather_fusion = bf16[4,2,128,5,128]{4,3,2,1,0:T(8,128)(2,1)S(1)} fusion(bf16[36,2,128,5,128]{4,3,2,1,0:T(8,128)(2,1)} %get-tuple-element.436, s32[1024]{0:T(1024)S(1)} %pad_clamp_fusion.2), kind=kCustom, calls=%fused_computation.clone.1 | custom fusion | bytes 2621456 | tf_op jit(solution)/shard_map/while/body/eval_jaxpr/while/body/jit(_take)/gather | solution.py:50
  502.4 51.1 %while.59 = (s32[]{:T(128)}, f32[5,128]{1,0:T(8,128)S(1)}, f32[5,128]{1,0:T(8,128)S(1)}, f32[128,5,128]{0,2,1:T(8,128)S(1)}, s32[]{:T(128)}, /*index=5*/s32[]{:T...) while((s32[]{:T(128)}, f32[5,128]{1,0:T(8,128)S(1)}, ...), condition=%wide.region_12.12_spmd, body=%wide.region_9.11_spmd.sunk | while | flops 171543456 | bytes 15284487 | solution.py:60
  503.1 7.3 %gather_fusion = bf16[4,2,128,5,128]{4,3,2,1,0:T(8,128)(2,1)S(1)} fusion(bf16[36,2,128,5,128]{4,3,2,1,0:T(8,128)(2,1)} %get-tuple-element.436, s32[1024]{0:T(1024)S(1)} %pad_clamp_fusion.2), kind=kCustom, calls=%fused_computation.clone.1 | custom fusion | bytes 2621456 | tf_op jit(solution)/shard_map/while/body/eval_jaxpr/while/body/jit(_take)/gather | solution.py:50
  513.3 7.3 %gather_fusion = bf16[4,2,128,5,128]{4,3,2,1,0:T(8,128)(2,1)S(1)} fusion(bf16[36,2,128,5,128]{4,3,2,1,0:T(8,128)(2,1)} %get-tuple-element.436, s32[1024]{0:T(1024)S(1)} %pad_clamp_fusion.2), kind=kCustom, calls=%fused_computation.clone.1 | custom fusion | bytes 2621456 | tf_op jit(solution)/shard_map/while/body/eval_jaxpr/while/body/jit(_take)/gather | solution.py:50
  523.5 7.3 %gather_fusion = bf16[4,2,128,5,128]{4,3,2,1,0:T(8,128)(2,1)S(1)} fusion(bf16[36,2,128,5,128]{4,3,2,1,0:T(8,128)(2,1)} %get-tuple-element.436, s32[1024]{0:T(1024)S(1)} %pad_clamp_fusion.2), kind=kCustom, calls=%fused_computation.clone.1 | custom fusion | bytes 2621456 | tf_op jit(solution)/shard_map/while/body/eval_jaxpr/while/body/jit(_take)/gather | solution.py:50
  533.7 7.3 %gather_fusion = bf16[4,2,128,5,128]{4,3,2,1,0:T(8,128)(2,1)S(1)} fusion(bf16[36,2,128,5,128]{4,3,2,1,0:T(8,128)(2,1)} %get-tuple-element.436, s32[1024]{0:T(1024)S(1)} %pad_clamp_fusion.2), kind=kCustom, calls=%fused_computation.clone.1 | custom fusion | bytes 2621456 | tf_op jit(solution)/shard_map/while/body/eval_jaxpr/while/body/jit(_take)/gather | solution.py:50
  543.9 7.3 %gather_fusion = bf16[4,2,128,5,128]{4,3,2,1,0:T(8,128)(2,1)S(1)} fusion(bf16[36,2,128,5,128]{4,3,2,1,0:T(8,128)(2,1)} %get-tuple-element.436, s32[1024]{0:T(1024)S(1)} %pad_clamp_fusion.2), kind=kCustom, calls=%fused_computation.clone.1 | custom fusion | bytes 2621456 | tf_op jit(solution)/shard_map/while/body/eval_jaxpr/while/body/jit(_take)/gather | solution.py:50
  556.3 51.0 %while.59 = (s32[]{:T(128)}, f32[5,128]{1,0:T(8,128)S(1)}, f32[5,128]{1,0:T(8,128)S(1)}, f32[128,5,128]{0,2,1:T(8,128)S(1)}, s32[]{:T(128)}, /*index=5*/s32[]{:T...) while((s32[]{:T(128)}, f32[5,128]{1,0:T(8,128)S(1)}, ...), condition=%wide.region_12.12_spmd, body=%wide.region_9.11_spmd.sunk | while | flops 171543456 | bytes 15284487 | solution.py:60
  557.0 7.3 %gather_fusion = bf16[4,2,128,5,128]{4,3,2,1,0:T(8,128)(2,1)S(1)} fusion(bf16[36,2,128,5,128]{4,3,2,1,0:T(8,128)(2,1)} %get-tuple-element.436, s32[1024]{0:T(1024)S(1)} %pad_clamp_fusion.2), kind=kCustom, calls=%fused_computation.clone.1 | custom fusion | bytes 2621456 | tf_op jit(solution)/shard_map/while/body/eval_jaxpr/while/body/jit(_take)/gather | solution.py:50
  567.2 7.3 %gather_fusion = bf16[4,2,128,5,128]{4,3,2,1,0:T(8,128)(2,1)S(1)} fusion(bf16[36,2,128,5,128]{4,3,2,1,0:T(8,128)(2,1)} %get-tuple-element.436, s32[1024]{0:T(1024)S(1)} %pad_clamp_fusion.2), kind=kCustom, calls=%fused_computation.clone.1 | custom fusion | bytes 2621456 | tf_op jit(solution)/shard_map/while/body/eval_jaxpr/while/body/jit(_take)/gather | solution.py:50
  577.4 7.3 %gather_fusion = bf16[4,2,128,5,128]{4,3,2,1,0:T(8,128)(2,1)S(1)} fusion(bf16[36,2,128,5,128]{4,3,2,1,0:T(8,128)(2,1)} %get-tuple-element.436, s32[1024]{0:T(1024)S(1)} %pad_clamp_fusion.2), kind=kCustom, calls=%fused_computation.clone.1 | custom fusion | bytes 2621456 | tf_op jit(solution)/shard_map/while/body/eval_jaxpr/while/body/jit(_take)/gather | solution.py:50
  587.7 7.3 %gather_fusion = bf16[4,2,128,5,128]{4,3,2,1,0:T(8,128)(2,1)S(1)} fusion(bf16[36,2,128,5,128]{4,3,2,1,0:T(8,128)(2,1)} %get-tuple-element.436, s32[1024]{0:T(1024)S(1)} %pad_clamp_fusion.2), kind=kCustom, calls=%fused_computation.clone.1 | custom fusion | bytes 2621456 | tf_op jit(solution)/shard_map/while/body/eval_jaxpr/while/body/jit(_take)/gather | solution.py:50
  610.3 51.1 %while.59 = (s32[]{:T(128)}, f32[5,128]{1,0:T(8,128)S(1)}, f32[5,128]{1,0:T(8,128)S(1)}, f32[128,5,128]{0,2,1:T(8,128)S(1)}, s32[]{:T(128)}, /*index=5*/s32[]{:T...) while((s32[]{:T(128)}, f32[5,128]{1,0:T(8,128)S(1)}, ...), condition=%wide.region_12.12_spmd, body=%wide.region_9.11_spmd.sunk | while | flops 171543456 | bytes 15284487 | solution.py:60
  631.4 7.3 %gather_fusion = bf16[4,2,128,5,128]{4,3,2,1,0:T(8,128)(2,1)S(1)} fusion(bf16[36,2,128,5,128]{4,3,2,1,0:T(8,128)(2,1)} %get-tuple-element.436, s32[1024]{0:T(1024)S(1)} %pad_clamp_fusion.2), kind=kCustom, calls=%fused_computation.clone.1 | custom fusion | bytes 2621456 | tf_op jit(solution)/shard_map/while/body/eval_jaxpr/while/body/jit(_take)/gather | solution.py:50
  664.5 15.2 %all_to_all.76 = bf16[8,64,640]{2,1,0:T(8,128)(2,1)S(1)} all-to-all(bf16[8,64,640]{2,1,0:T(8,128)(2,1)S(1)} %all_to_all.67), channel_id=1, replica_groups=mesh['seq'=32,'head'=8] {'head'}, dimensions={0} | all-to-all | bytes 1310720 | tf_op jit(solution)/shard_map/all_to_all | solution.py:138
  (330 shorter events, 131.8 us)
Async XLA Ops:
  2.7 6.9 %copy-start.2 = (bf16[64,5120]{1,0:T(8,128)(2,1)S(1)}, bf16[64,5120]{1,0:T(8,128)(2,1)}, u32[]{:S(2)}) copy-start(bf16[64,5120]{1,0:T(8,128)(2,1)} %param.13) | copy-start | bytes 1966084
  3.6 6.9 %copy-start = (bf16[64,5120]{1,0:T(8,128)(2,1)S(1)}, bf16[64,5120]{1,0:T(8,128)(2,1)}, u32[]{:S(2)}) copy-start(bf16[64,5120]{1,0:T(8,128)(2,1)} %param.11) | copy-start | bytes 1966084
  3.6 16.6 %all-to-all-start.1 = ((bf16[64,8,640]{2,0,1:T(8,128)(2,1)}), bf16[64,8,640]{2,0,1:T(8,128)(2,1)S(1)}, u32[]{:S(2)}, u32[]{:S(2)}) async-start(bf16[64,8,640]{2,0,1:T(8,128)(2,1)} %bitcast.42), calls=%async_computation.1 | async-start | bytes 1310720 | tf_op jit(solution)/shard_map/all_to_all | solution.py:95
  10.4 13.3 %copy-start.4 = (f32[5120]{0:T(1024)S(1)}, f32[5120]{0:T(1024)}, u32[]{:S(2)}) copy-start(f32[5120]{0:T(1024)} %param.14) | copy-start | bytes 61444
  20.2 14.4 %all-to-all-start.2 = ((bf16[64,8,640]{2,0,1:T(8,128)(2,1)}), bf16[64,8,640]{2,0,1:T(8,128)(2,1)S(1)}, u32[]{:S(2)}, u32[]{:S(2)}) async-start(bf16[64,8,640]{2,0,1:T(8,128)(2,1)} %bitcast.41), calls=%async_computation.2 | async-start | bytes 1310720 | tf_op jit(solution)/shard_map/all_to_all | solution.py:96
  24.0 14.2 %copy-start.5 = (s32[128]{0:T(128)S(1)}, s32[128]{0:T(128)}, u32[]{:S(2)}) copy-start(s32[128]{0:T(128)} %param.17) | copy-start | bytes 1540
  24.0 14.2 %copy-start.3 = (s32[128,20]{0,1:T(8,128)S(1)}, s32[128,20]{0,1:T(8,128)}, u32[]{:S(2)}) copy-start(s32[128,20]{0,1:T(8,128)} %param.16) | copy-start | bytes 30724
  34.6 42.0 %all-to-all-start = ((bf16[64,8,640]{2,0,1:T(8,128)(2,1)}), bf16[64,8,640]{2,0,1:T(8,128)(2,1)S(1)}, u32[]{:S(2)}, u32[]{:S(2)}) async-start(bf16[64,8,640]{2,0,1:T(8,128)(2,1)} %bitcast.43), calls=%async_computation | async-start | bytes 1310720 | tf_op jit(solution)/shard_map/all_to_all | solution.py:94
  76.6 0.8 copy-start.1
  77.5 242.4 %all-to-all-start.3 = ((bf16[32,2,81920]{2,1,0:T(2,128)(2,1)}), bf16[32,2,81920]{2,1,0:T(2,128)(2,1)}, u32[]{:S(2)}, u32[]{:S(2)}) async-start(bf16[32,2,81920]{2,1,0:T(2,128)(2,1)} %reshape.156), calls=%async_computation.3 | async-start | bytes 20971520 | tf_op jit(solution)/shard_map/all_to_all | solution.py:85
where the time goes:
time: 683 us; the launch traced here: 681 us
  waiting for transfers between devices  245 us (36%)
  local copies, waits for them, and re-layouts  235 us (34%)
  other arithmetic  127 us (19%)
  matrix products  29.7 us (4%)
  starting transfers between devices  23.8 us (3%)
  blocking collectives  15.2 us (2%)
    all_to_all x1, waiting for transfers between devices, fetch_tiles(): lax.all_to_all(outgoing, 'seq', split_axis=0, concat_axis=0, tiled=True)  226 us
    gather x20, local copies, waits for them, and re-layouts, advance(): chosen = jnp.take(kv_source, picked, axis=0)  146 us
    all_to_all x2, other arithmetic, fetch_tiles(): lax.all_to_all(outgoing, 'seq', split_axis=0, concat_axis=0, tiled=True)  76.8 us
    unnamed x14, local copies, waits for them, and re-layouts  39.5 us
    reshape x1, local copies, waits for them, and re-layouts, local(): far_pool = received.reshape(group_total * CAP, 2, TILE, head_count, HD)  19.3 us
    concatenate x1, other arithmetic, local(): kv_pool = jnp.concatenate([near_pool, far_pool], axis=0)  18 us
    all_to_all x1, blocking collectives, local(): lax.all_to_all(attended, 'head', split_axis=0, concat_axis=1, tiled=True)  15.2 us
  transfers between devices with their start and end apart: 4, of which 3 were waited for; matrix products, arithmetic and copies ran while one was open for 7% of the time, Pallas kernels for 0%

commit v1 on v0

v1 whole, which is shorter than its diff:
```python
import jax
import jax.numpy as jnp
from jax import lax
from jax.experimental import pallas as pl
from jax.experimental.pallas import tpu as pltpu
from jax.sharding import PartitionSpec as P

HD = 128
TILE = 128
HALF = 64
HEADS = 40
NX, NY, NZ, NC = 4, 4, 8, 2
SLICE = HEADS // NZ
LIST = 20
SURE = 12
UNITS = 20
BLOCKS = NC * NZ * NX
MESH = pl.DeviceIdType.MESH
OFFSETS = (0, 1, 7, 2, 6, 3, 5, 4)


def place():
    seq = lax.axis_index("seq")
    head = lax.axis_index("head")
    c = lax.rem(seq, 2)
    x = lax.rem(lax.div(seq, 2), NX)
    z_hi = lax.div(seq, 2 * NX)
    z_lo = lax.div(head, NY)
    y = lax.rem(head, NY)
    return x, y, 2 * z_hi + z_lo, c


def device(x, y, z, c):
    return ((lax.div(z, 2) * NX + x) * 2 + c, lax.rem(z, 2) * NY + y)


def send(src, dst, send_sem, recv_sem, target):
    pltpu.make_async_remote_copy(
        src_ref=src,
        dst_ref=dst,
        send_sem=send_sem,
        recv_sem=recv_sem,
        device_id=target,
        device_id_type=MESH,
    ).start()


def await_bytes(ref, sem):
    pltpu.make_async_copy(ref, ref, sem).wait()


def normalize_into(src, gain, dst_of_head):
    def rows(block, _):
        span = pl.ds(pl.multiple_of(block * 16, 16), 16)
        values = src[span, :].astype(jnp.float32)
        square_mean = jnp.mean(values * values, axis=1, keepdims=True)
        scale = lax.rsqrt(square_mean + 1e-06)
        for h in range(HEADS):
            cols = slice(h * HD, (h + 1) * HD)
            part = src[span, cols].astype(jnp.float32) * scale * gain[:, cols]
            dst_of_head(h, span, part.astype(jnp.bfloat16))
        return 0

    lax.fori_loop(0, HALF // 16, rows, 0)


def exchange_kernel(
    q_ref, k_ref, v_ref, qg_ref, kg_ref, row_kv, all_kv, queries,
    pack_kv, pack_q, z_send, x_send, y_send, mate_send, q_send,
    zr_recv, z4_recv, xr_recv, x4_recv, y4_recv, mate_recv, q_recv,
):
    x, y, z, c = place()
    barrier = pltpu.get_barrier_semaphore()
    partners = []
    for dz in range(NZ):
        for dy in range(NY):
            if dz or dy:
                partners.append(device(x, lax.rem(y + dy, NY), lax.rem(z + dz, NZ), c))
    right = device(lax.rem(x + 1, NX), y, z, c)
    left = device(lax.rem(x + NX - 1, NX), y, z, c)
    up = device(x, lax.rem(y + 1, NY), z, c)
    down = device(x, lax.rem(y + NY - 1, NY), z, c)
    mate = device(x, y, z, 1 - c)
    partners += [right, left, mate]
    for target in partners:
        pl.semaphore_signal(barrier, inc=1, device_id=target, device_id_type=MESH)

    def put_k(h, span, part):
        pack_kv[h, 0, span, :] = part

    def put_q(h, span, part):
        pack_q[h, span, :] = part

    normalize_into(k_ref, kg_ref, put_k)
    for h in range(HEADS):
        pack_kv[h, 1] = v_ref[:, h * HD:(h + 1) * HD]

    pl.semaphore_wait(barrier, len(partners))

    block = (c * NZ + z) * NX + x
    for i, dz in enumerate(OFFSETS):
        zd = lax.rem(z + dz, NZ)
        for dy in range(NY):
            yd = lax.rem(y + dy, NY)
            src = pack_kv.at[SLICE * zd + yd]
            dst = row_kv.at[block, :, y]
            if dz or dy:
                send(src, dst, z_send.at[0], zr_recv.at[i], device(x, yd, zd, c))
            else:
                pltpu.make_async_copy(src, dst, zr_recv.at[i]).start()
        src = pack_kv.at[SLICE * zd + NY]
        dst = all_kv.at[block, :, y]
        if dz:
            send(src, dst, z_send.at[0], z4_recv.at[i], device(x, y, zd, c))
        else:
            pltpu.make_async_copy(src, dst, z4_recv.at[i]).start()

    normalize_into(q_ref, qg_ref, put_q)
    z_hi, z_lo = lax.div(z, 2), lax.rem(z, 2)
    for i, dz in enumerate(OFFSETS):
        zd = lax.rem(z + dz, NZ)
        for dy in range(NY):
            yd = lax.rem(y + dy, NY)
            src = pack_q.at[SLICE * zd + yd]
            dst = queries.at[z * NY + y]
            if dz or dy:
                send(src, dst, q_send.at[0], q_recv.at[0], device(x, yd, zd, c))
            else:
                pltpu.make_async_copy(src, dst, q_recv.at[0]).start()
        src = pack_q.at[SLICE * zd + NY]
        dst = queries.at[NZ * NY + z_lo * NY + y]
        if dz:
            send(src, dst, q_send.at[0], q_recv.at[0], device(x, z_hi, zd, c))
        else:
            @pl.when(z_hi == y)
            def _(src=src, dst=dst):
                pltpu.make_async_copy(src, dst, q_recv.at[0]).start()

            @pl.when(z_hi != y)
            def _(src=src, dst=dst, zd=zd):
                send(src, dst, q_send.at[1], q_recv.at[0], device(x, z_hi, zd, c))

    x_left, x_right, x_far = lax.rem(x + NX - 1, NX), lax.rem(x + 1, NX), lax.rem(x + 2, NX)
    y_down, y_up, y_far = lax.rem(y + NY - 1, NY), lax.rem(y + 1, NY), lax.rem(y + 2, NY)

    def first(i):
        return (c * NZ + lax.rem(z + NZ - OFFSETS[i], NZ)) * NX

    def own_along_x(i):
        mine = row_kv.at[first(i) + x]
        await_bytes(mine, zr_recv.at[i])
        send(mine, mine, x_send.at[0], xr_recv.at[0, i], right)
        send(mine, mine, x_send.at[0], xr_recv.at[1, i], left)
        mine = all_kv.at[first(i) + x, :, y]
        await_bytes(mine, z4_recv.at[i])
        send(mine, mine, x_send.at[1], x4_recv.at[0, i], right)
        send(mine, mine, x_send.at[1], x4_recv.at[1, i], left)

    def far_along_x(i):
        from_left = row_kv.at[first(i) + x_left]
        from_right = row_kv.at[first(i) + x_right]
        await_bytes(from_left, xr_recv.at[0, i])
        await_bytes(from_right, xr_recv.at[1, i])
        if i % 2 == 0:
            send(from_left, from_left, x_send.at[0], xr_recv.at[2, i], right)
        else:
            send(from_right, from_right, x_send.at[0], xr_recv.at[2, i], left)
        from_left = all_kv.at[first(i) + x_left, :, y]
        from_right = all_kv.at[first(i) + x_right, :, y]
        await_bytes(from_left, x4_recv.at[0, i])
        await_bytes(from_right, x4_recv.at[1, i])
        if i % 2 == 0:
            send(from_left, from_left, x_send.at[1], x4_recv.at[2, i], right)
        else:
            send(from_right, from_right, x_send.at[1], x4_recv.at[2, i], left)

    def own_along_y(i):
        await_bytes(all_kv.at[first(i) + x_far, :, y], x4_recv.at[2, i])
        mine = all_kv.at[pl.ds(first(i), NX), :, y]
        send(mine, mine, y_send.at[0], y4_recv.at[0, i], up)
        send(mine, mine, y_send.at[0], y4_recv.at[1, i], down)
        await_bytes(row_kv.at[first(i) + x_far], xr_recv.at[2, i])
        whole = row_kv.at[pl.ds(first(i), NX)]
        send(whole, whole, mate_send.at[0], mate_recv.at[0], mate)

    def far_along_y(i):
        from_down = all_kv.at[pl.ds(first(i), NX), :, y_down]
        from_up = all_kv.at[pl.ds(first(i), NX), :, y_up]
        await_bytes(from_down, y4_recv.at[0, i])
        await_bytes(from_up, y4_recv.at[1, i])
        if i % 2 == 0:
            send(from_down, from_down, y_send.at[0], y4_recv.at[2, i], up)
        else:
            send(from_up, from_up, y_send.at[0], y4_recv.at[2, i], down)

    def to_mate(i):
        await_bytes(all_kv.at[pl.ds(first(i), NX), :, y_far], y4_recv.at[2, i])
        whole = all_kv.at[pl.ds(first(i), NX)]
        send(whole, whole, mate_send.at[1], mate_recv.at[1], mate)

    stages = ((6, to_mate), (5, far_along_y), (3, own_along_y), (2, far_along_x), (0, own_along_x))
    for step in range(NZ + 6):
        for lag, stage in stages:
            if 0 <= step - lag < NZ:
                stage(step - lag)

    other = row_kv.at[pl.ds((1 - c) * NZ * NX, NZ * NX)]
    await_bytes(other, mate_recv.at[0])
    other = all_kv.at[pl.ds((1 - c) * NZ * NX, NZ * NX)]
    await_bytes(other, mate_recv.at[1])
    await_bytes(queries, q_recv.at[0])

    await_bytes(pack_kv.at[pl.ds(0, NZ * NY - 1 + NZ - 1)], z_send.at[0])
    await_bytes(pack_q.at[pl.ds(0, NZ * NY - 1 + NZ - 1)], q_send.at[0])

    @pl.when(z_hi != y)
    def _():
        await_bytes(pack_q.at[0], q_send.at[1])

    await_bytes(row_kv.at[pl.ds(0, 3 * NZ)], x_send.at[0])
    await_bytes(all_kv.at[pl.ds(0, 3 * NZ), :, 0], x_send.at[1])
    await_bytes(all_kv.at[pl.ds(0, 3 * NZ)], y_send.at[0])
    await_bytes(row_kv.at[pl.ds(0, NX * NZ)], mate_send.at[0])
    await_bytes(all_kv.at[pl.ds(0, NX * NZ)], mate_send.at[1])


def exchange(query, key_in, value, query_gain, key_gain):
    kv_type = jax.ShapeDtypeStruct((BLOCKS, 2, NY, HALF, HD), jnp.bfloat16)
    q_type = jax.ShapeDtypeStruct((2 * UNITS, HALF, HD), jnp.bfloat16)
    vmem = pl.BlockSpec(memory_space=pltpu.VMEM)
    hbm = pl.BlockSpec(memory_space=pl.ANY)
    dma = pltpu.SemaphoreType.DMA
    return pl.pallas_call(
        exchange_kernel,
        out_shape=(kv_type, kv_type, q_type),
        in_specs=[vmem] * 5,
        out_specs=(hbm, hbm, hbm),
        scratch_shapes=[
            pltpu.VMEM((HEADS, 2, HALF, HD), jnp.bfloat16),
            pltpu.VMEM((HEADS, HALF, HD), jnp.bfloat16),
            dma((1,)), dma((2,)), dma((1,)), dma((2,)), dma((2,)),
            dma((NZ,)), dma((NZ,)), dma((3, NZ)), dma((3, NZ)), dma((3, NZ)), dma((2,)), dma((1,)),
        ],
        compiler_params=pltpu.CompilerParams(
            collective_id=0, has_side_effects=True, vmem_limit_bytes=32 * 2**20
        ),
        name="exchange",
    )(query, key_in, value, query_gain.reshape(1, -1), key_gain.reshape(1, -1))


def attend_kernel(lists, lengths, row_kv, all_kv, q_ref, out_ref, scores):
    x, y, z, c = place()
    scale = HD ** (-0.5)

    def unit(kv, u, group_tile):
        length = lengths[group_tile]
        q_tile = q_ref[u]

        def tile_at(n):
            entry = lists[n, group_tile]
            z = ((entry >> 5) << 1) + ((entry >> 1) & 1)
            block = ((((entry >> 2) & 1) * NZ) + z) * NX + ((entry >> 3) & 3)
            return block, entry & 1

        def score(n):
            block, a = tile_at(n)
            keys = kv[block, 0, a]
            return lax.dot_general(
                q_tile, keys, (((1,), (1,)), ((), ())), preferred_element_type=jnp.float32
            )

        high = None
        for n in range(SURE):
            s = score(n)
            scores[n] = s
            high = s if high is None else jnp.maximum(high, s)
        scores_high = high

        def more_scores(n, high):
            s = score(n)
            scores[n] = s
            return jnp.maximum(high, s)

        high = lax.fori_loop(SURE, length, more_scores, scores_high)
        row_high = jnp.max(high, axis=1, keepdims=True) * scale

        def weigh(n, total, acc):
            block, a = tile_at(n)
            raw = jnp.exp(scores[n] * scale - row_high)
            mixed = jnp.dot(
                raw.astype(jnp.bfloat16), kv[block, 1, a],
                preferred_element_type=jnp.float32,
            )
            return total + raw, acc + mixed

        total = jnp.zeros((TILE, TILE), jnp.float32)
        acc = jnp.zeros((TILE, HD), jnp.float32)
        for n in range(SURE):
            total, acc = weigh(n, total, acc)
        total, acc = lax.fori_loop(
            SURE, length, lambda n, state: weigh(n, *state), (total, acc)
        )
        summed = jnp.sum(total, axis=1, keepdims=True)
        out_ref[u] = (acc / summed).astype(jnp.bfloat16)

    def row_unit(u, _):
        unit(row_kv, u, (((u >> 2) * NX + x) * 2 + c) * 4 + (u & 3))
        return 0

    lax.fori_loop(0, 16, row_unit, 0)

    def all_unit(v, _):
        unit(all_kv, 16 + v, ((y * NX + x) * 2 + c) * 4 + v)
        return 0

    lax.fori_loop(0, 4, all_unit, 0)


def attend(row_kv, all_kv, queries, tile_lists, list_lengths):
    smem = pl.BlockSpec(memory_space=pltpu.SMEM)
    vmem = pl.BlockSpec(memory_space=pltpu.VMEM)
    shape = (BLOCKS, 2, 2, TILE, HD)
    return pl.pallas_call(
        attend_kernel,
        out_shape=jax.ShapeDtypeStruct((UNITS, TILE, HD), jnp.bfloat16),
        in_specs=[smem, smem, vmem, vmem, vmem],
        out_specs=vmem,
        scratch_shapes=[
            pltpu.VMEM((LIST, TILE, TILE), jnp.float32),
        ],
        compiler_params=pltpu.CompilerParams(vmem_limit_bytes=24 * 2**20),
        name="attend",
    )(
        tile_lists.T, list_lengths,
        row_kv.reshape(shape), all_kv.reshape(shape), queries.reshape(UNITS, TILE, HD),
    )


def return_kernel(o_ref, out_ref, send_sem, recv_sem):
    x, y, z, c = place()
    barrier = pltpu.get_barrier_semaphore()
    count = 0
    for dz in range(NZ):
        for dy in range(NY):
            if dz or dy:
                target = device(x, lax.rem(y + dy, NY), lax.rem(z + dz, NZ), c)
                pl.semaphore_signal(barrier, inc=1, device_id=target, device_id_type=MESH)
                count += 1
    pl.semaphore_wait(barrier, count)

    columns = out_ref.at[:, pl.ds(pl.multiple_of((SLICE * z + y) * HD, HD), HD)]
    for dz in OFFSETS:
        zd = lax.rem(z + dz, NZ)
        for dy in range(NY):
            yd = lax.rem(y + dy, NY)
            src = o_ref.at[zd * NY + yd]
            if dz or dy:
                send(src, columns, send_sem.at[0], recv_sem.at[0], device(x, yd, zd, c))
            else:
                pltpu.make_async_copy(src, columns, recv_sem.at[0]).start()
    columns = out_ref.at[:, pl.ds(pl.multiple_of((SLICE * z + NY) * HD, HD), HD)]
    for z_lo in range(2):
        zd = 2 * y + z_lo
        for dy in range(NY):
            yd = lax.rem(y + dy, NY)
            src = o_ref.at[NZ * NY + z_lo * NY + yd]
            if dy:
                send(src, columns, send_sem.at[0], recv_sem.at[0], device(x, yd, zd, c))
            else:
                @pl.when(zd == z)
                def _(src=src):
                    pltpu.make_async_copy(src, columns, recv_sem.at[0]).start()

                @pl.when(zd != z)
                def _(src=src, yd=yd, zd=zd, z_lo=z_lo):
                    send(src, columns, send_sem.at[1 + z_lo], recv_sem.at[0], device(x, yd, zd, c))

    await_bytes(out_ref, recv_sem.at[0])
    await_bytes(o_ref.at[pl.ds(0, NZ * NY - 1 + 2 * (NY - 1))], send_sem.at[0])
    for z_lo in range(2):
        @pl.when(2 * y + z_lo != z)
        def _(z_lo=z_lo):
            await_bytes(o_ref.at[0], send_sem.at[1 + z_lo])


def give_back(attended):
    hbm = pl.BlockSpec(memory_space=pl.ANY)
    dma = pltpu.SemaphoreType.DMA
    return pl.pallas_call(
        return_kernel,
        out_shape=jax.ShapeDtypeStruct((HALF, HEADS * HD), jnp.bfloat16),
        in_specs=[pl.BlockSpec(memory_space=pltpu.VMEM)],
        out_specs=hbm,
        scratch_shapes=[dma((3,)), dma((1,))],
        compiler_params=pltpu.CompilerParams(
            collective_id=1, has_side_effects=True, vmem_limit_bytes=8 * 2**20
        ),
        name="give_back",
    )(attended.reshape(2 * UNITS, HALF, HD))


def local(query, key_in, value, query_gain, key_gain, tile_lists, list_lengths):
    row_kv, all_kv, queries = exchange(query, key_in, value, query_gain, key_gain)
    attended = attend(row_kv, all_kv, queries, tile_lists, list_lengths)
    return give_back(attended)


def solution(mesh):
    in_specs = (
        P(("seq", "head"), None),
        P(("seq", "head"), None),
        P(("seq", "head"), None),
        P(),
        P(),
        P(),
        P(),
    )
    out_specs = P(("seq", "head"), None)
    return jax.shard_map(local, mesh=mesh, in_specs=in_specs, out_specs=out_specs, check_vma=False)
```

time: 683 us -> 154 us (0.23)
  the two profiles are of different devices: /device:TPU:6 before, /device:TPU:56 now
where the time goes in v1:
time: 154 us; the launch traced here: 152 us
  Pallas kernels  145 us (94%)
  local copies, waits for them, and re-layouts  6.91 us (4%)
    pallas_call x1, Pallas kernels, exchange(): pl.pallas_call(exchange_kernel, out_shape=(kv_type, kv_type, q_type), in_...  82.2 us
    pallas_call x1, Pallas kernels, give_back(): pl.pallas_call(return_kernel, out_shape=jax.ShapeDtypeStruct((HALF, HEADS...  33.9 us
    pallas_call x1, Pallas kernels, attend(): pl.pallas_call(attend_kernel, out_shape=jax.ShapeDtypeStruct((UNITS, TILE...  28.8 us
    unnamed x15, local copies, waits for them, and re-layouts  6.91 us

profile of v1, /device:TPU:56, one launch (start us, length us, event | category | flops | bytes accessed | tf_op | source)
XLA Modules:
  0.0 151.8 jit_solution(11456679152087943943)
XLA Ops:
  0.0 0.0 copy-start
  0.0 1.1 copy-done
  1.1 0.0 copy-start.1
  1.1 1.1 copy-done.1
  2.2 0.0 copy-start.2
  2.2 1.1 copy-done.2
  3.3 0.0 copy-start.3
  3.3 0.7 copy-done.3
  4.0 0.0 copy-start.4
  4.0 0.7 copy-done.4
  4.7 82.2 %exchange.1 = (bf16[64,2,4,64,128]{4,3,2,1,0:T(8,128)(2,1)S(1)}, bf16[64,2,4,64,128]{4,3,2,1,0:T(8,128)(2,1)S(1)}, bf16[40,64,128]{2,1,0:T(8,128)(2,1)S(1)}) custom-call(bf16[64,5120]{1,0:T(8,128)(2,1)S(1)} %copy-done, bf16[64,5120]{1,0:T(8,128)(2,1)S(1)} %copy-done.1, bf16[64,5120]{1,0:T(8,128)(2,1)S(1)} %copy-done.2, f32[1,5120]{1,0:T(1,128)S(1)} %bitcast.11, ...), custom_call_target="tpu_custom_call" | custom-call | tf_op jit(solution)/shard_map/exchange/pallas_call | solution.py:233
  86.9 0.0 copy-start.5
  86.9 0.7 copy-done.5
  87.6 0.0 copy-start.6
  87.6 0.7 copy-done.6
  88.2 28.8 %attend.1 = bf16[20,128,128]{2,1,0:T(8,128)(2,1)S(1)} custom-call(s32[20,128]{1,0:T(8,128)S(1)} %bitcast.13, s32[128]{0:T(128)S(1)} %copy-done.6, bf16[64,2,2,128,128]{4,3,2,1,0:T(8,128)(2,1)S(1)} %bitcast.7, bf16[64,2,2,128,128]{4,3,2,1,0:T(8,128)(2,1)S(1)} %bitcast.8, bf16[20,128,128]{2,1,0:T(8,128)(2,1)S(1)} %bitcast.10), custom_call_target="tpu_custom_call" | custom-call | tf_op jit(solution)/shard_map/attend/pallas_call | solution.py:323
  117.1 33.9 %give_back.1 = bf16[64,5120]{1,0:T(8,128)(2,1)S(1)} custom-call(bf16[40,64,128]{2,1,0:T(8,128)(2,1)S(1)} %bitcast.9), custom_call_target="tpu_custom_call" | custom-call | tf_op jit(solution)/shard_map/give_back/pallas_call | solution.py:389
  151.0 0.8 copy.9
Async XLA Ops:
  0.0 1.1 copy-start
  1.1 1.1 copy-start.1
  2.2 1.1 copy-start.2
  3.3 0.7 copy-start.3
  4.0 0.7 copy-start.4
  86.9 0.7 copy-start.5
  87.6 0.7 copy-start.6

commit v2 on v1

v2 whole, which is shorter than its diff:
```python
import math

import jax
import jax.numpy as jnp
from jax import lax
from jax.experimental import pallas as pl
from jax.experimental.pallas import tpu as pltpu
from jax.sharding import PartitionSpec as P

HD = 128
TILE = 128
HALF = 64
HEADS = 40
NX, NY, NZ, NC = 4, 4, 8, 2
SLICE = HEADS // NZ
LIST = 20
SURE = 12
PAIR = 2
LOG2_SCALE = HD ** (-0.5) * math.log2(math.e)
UNITS = 20
BLOCKS = NC * NZ * NX
MESH = pl.DeviceIdType.MESH
OFFSETS = (0, 1, 7, 2, 6, 3, 5, 4)


def place():
    seq = lax.axis_index("seq")
    head = lax.axis_index("head")
    c = lax.rem(seq, 2)
    x = lax.rem(lax.div(seq, 2), NX)
    z_hi = lax.div(seq, 2 * NX)
    z_lo = lax.div(head, NY)
    y = lax.rem(head, NY)
    return x, y, 2 * z_hi + z_lo, c


def device(x, y, z, c):
    return ((lax.div(z, 2) * NX + x) * 2 + c, lax.rem(z, 2) * NY + y)


def send(src, dst, send_sem, recv_sem, target):
    pltpu.make_async_remote_copy(
        src_ref=src,
        dst_ref=dst,
        send_sem=send_sem,
        recv_sem=recv_sem,
        device_id=target,
        device_id_type=MESH,
    ).start()


def await_bytes(ref, sem):
    pltpu.make_async_copy(ref, ref, sem).wait()


def normalize_into(src, gain, dst_of_head):
    def rows(block, _):
        span = pl.ds(pl.multiple_of(block * 16, 16), 16)
        squares = jnp.zeros((16, HD), jnp.float32)
        for h in range(HEADS):
            part = src[span, h * HD:(h + 1) * HD].astype(jnp.float32)
            squares = squares + part * part
        square_mean = jnp.sum(squares, axis=1, keepdims=True) * (1.0 / (HEADS * HD))
        scale = lax.rsqrt(square_mean + 1e-06)
        for h in range(HEADS):
            cols = slice(h * HD, (h + 1) * HD)
            part = src[span, cols].astype(jnp.float32) * scale * gain[:, cols]
            dst_of_head(h, span, part.astype(jnp.bfloat16))
        return 0

    lax.fori_loop(0, HALF // 16, rows, 0)


def attend_unit(kv, q_tile, out_ref, out_index, lists, row, length, scores):
    at = []
    for n in range(LIST):
        entry = lists[n, row]
        z = ((entry >> 5) << 1) + ((entry >> 1) & 1)
        at.append(((((entry >> 2) & 1) * NZ + z) * NX + ((entry >> 3) & 3), entry & 1))
    high = None
    for n in range(0, LIST, PAIR):
        keys = jnp.concatenate(
            [kv[at[m][0], 0, pl.ds(2 * at[m][1], 2)].reshape(TILE, HD) for m in range(n, n + PAIR)], axis=0
        )
        both = lax.dot_general(
            q_tile, keys, (((1,), (1,)), ((), ())), preferred_element_type=jnp.float32
        )
        for m in range(n, n + PAIR):
            s = both[:, (m - n) * TILE:(m - n + 1) * TILE]
            if m >= SURE:
                s = jnp.where(m < length, s, -1e30)
            scores[m] = s
            high = s if high is None else jnp.maximum(high, s)
    row_high = jnp.max(high, axis=1, keepdims=True)
    total = None
    acc = None
    for n in range(0, LIST, PAIR):
        weights = []
        for m in range(n, n + PAIR):
            raw = jnp.exp2((scores[m] - row_high) * LOG2_SCALE)
            total = raw if total is None else total + raw
            weights.append(raw.astype(jnp.bfloat16))
        values = jnp.concatenate(
            [kv[at[m][0], 1, pl.ds(2 * at[m][1], 2)].reshape(TILE, HD) for m in range(n, n + PAIR)], axis=0
        )
        mixed = jnp.dot(
            jnp.concatenate(weights, axis=1), values, preferred_element_type=jnp.float32
        )
        acc = mixed if acc is None else acc + mixed
    summed = jnp.sum(total, axis=1, keepdims=True)
    out_ref[out_index] = (acc / summed).astype(jnp.bfloat16).reshape(2, HALF, HD)


def fused_kernel(
    q_hbm, k_hbm, v_hbm, qg_hbm, kg_hbm, lists_hbm, lengths_hbm, out_ref,
    q_ref, k_ref, v_ref, qg_ref, kg_ref, lists, lengths,
    pack_kv, pack_q, row_kv, all_kv, queries, scores, results,
    load_sem, z_send, x_send, y_send, mate_send, q_send, out_send,
    zr_recv, z4_recv, xr_recv, x4_recv, y4_recv, mate_recv, q_recv, out_recv,
):
    loads = []
    for n, (src, dst) in enumerate((
        (k_hbm, k_ref), (kg_hbm, kg_ref), (v_hbm, v_ref), (q_hbm, q_ref), (qg_hbm, qg_ref),
        (lists_hbm, lists), (lengths_hbm, lengths),
    )):
        copy = pltpu.make_async_copy(src, dst, load_sem.at[n])
        copy.start()
        loads.append(copy)
    x, y, z, c = place()
    barrier = pltpu.get_barrier_semaphore()
    partners = []
    for dz in range(NZ):
        for dy in range(NY):
            if dz or dy:
                partners.append(device(x, lax.rem(y + dy, NY), lax.rem(z + dz, NZ), c))
    right = device(lax.rem(x + 1, NX), y, z, c)
    left = device(lax.rem(x + NX - 1, NX), y, z, c)
    up = device(x, lax.rem(y + 1, NY), z, c)
    down = device(x, lax.rem(y + NY - 1, NY), z, c)
    mate = device(x, y, z, 1 - c)
    partners += [right, left, mate]
    for target in partners:
        pl.semaphore_signal(barrier, inc=1, device_id=target, device_id_type=MESH)

    def put_k(h, span, part):
        pack_kv[h, 0, span, :] = part

    def put_q(h, span, part):
        pack_q[h, span, :] = part

    loads[0].wait()
    loads[1].wait()
    normalize_into(k_ref, kg_ref, put_k)
    loads[2].wait()
    for h in range(HEADS):
        pack_kv[h, 1] = v_ref[:, h * HD:(h + 1) * HD]

    pl.semaphore_wait(barrier, len(partners))

    block = (c * NZ + z) * NX + x
    for i, dz in enumerate(OFFSETS):
        zd = lax.rem(z + dz, NZ)
        for dy in range(NY):
            yd = lax.rem(y + dy, NY)
            src = pack_kv.at[SLICE * zd + yd]
            dst = row_kv.at[block, :, y]
            if dz or dy:
                send(src, dst, z_send.at[0], zr_recv.at[i], device(x, yd, zd, c))
            else:
                pltpu.make_async_copy(src, dst, zr_recv.at[i]).start()
        src = pack_kv.at[SLICE * zd + NY]
        dst = all_kv.at[block, :, y]
        if dz:
            send(src, dst, z_send.at[0], z4_recv.at[i], device(x, y, zd, c))
        else:
            pltpu.make_async_copy(src, dst, z4_recv.at[i]).start()

    loads[3].wait()
    loads[4].wait()
    normalize_into(q_ref, qg_ref, put_q)
    z_hi, z_lo = lax.div(z, 2), lax.rem(z, 2)
    for i, dz in enumerate(OFFSETS):
        zd = lax.rem(z + dz, NZ)
        for dy in range(NY):
            yd = lax.rem(y + dy, NY)
            src = pack_q.at[SLICE * zd + yd]
            dst = queries.at[z * NY + y]
            if dz or dy:
                send(src, dst, q_send.at[0], q_recv.at[0], device(x, yd, zd, c))
            else:
                pltpu.make_async_copy(src, dst, q_recv.at[0]).start()
        src = pack_q.at[SLICE * zd + NY]
        dst = queries.at[NZ * NY + z_lo * NY + y]
        if dz:
            send(src, dst, q_send.at[0], q_recv.at[0], device(x, z_hi, zd, c))
        else:
            @pl.when(z_hi == y)
            def _(src=src, dst=dst):
                pltpu.make_async_copy(src, dst, q_recv.at[0]).start()

            @pl.when(z_hi != y)
            def _(src=src, dst=dst, zd=zd):
                send(src, dst, q_send.at[1], q_recv.at[0], device(x, z_hi, zd, c))

    x_left, x_right, x_far = lax.rem(x + NX - 1, NX), lax.rem(x + 1, NX), lax.rem(x + 2, NX)
    y_down, y_up, y_far = lax.rem(y + NY - 1, NY), lax.rem(y + 1, NY), lax.rem(y + 2, NY)

    def first(i):
        return (c * NZ + lax.rem(z + NZ - OFFSETS[i], NZ)) * NX

    def own_along_x(i):
        mine = row_kv.at[first(i) + x]
        await_bytes(mine, zr_recv.at[i])
        send(mine, mine, x_send.at[0], xr_recv.at[0, i], right)
        send(mine, mine, x_send.at[0], xr_recv.at[1, i], left)

    def far_along_x(i):
        from_left = row_kv.at[first(i) + x_left]
        from_right = row_kv.at[first(i) + x_right]
        await_bytes(from_left, xr_recv.at[0, i])
        await_bytes(from_right, xr_recv.at[1, i])
        if i % 2 == 0:
            send(from_left, from_left, x_send.at[0], xr_recv.at[2, i], right)
        else:
            send(from_right, from_right, x_send.at[0], xr_recv.at[2, i], left)

    def to_mate(i):
        await_bytes(row_kv.at[first(i) + x_far], xr_recv.at[2, i])
        whole = row_kv.at[pl.ds(first(i), NX)]
        send(whole, whole, mate_send.at[0], mate_recv.at[0], mate)

    def own_along_x4(i):
        mine = all_kv.at[first(i) + x, :, y]
        await_bytes(mine, z4_recv.at[i])
        send(mine, mine, x_send.at[1], x4_recv.at[0, i], right)
        send(mine, mine, x_send.at[1], x4_recv.at[1, i], left)

    def far_along_x4(i):
        from_left = all_kv.at[first(i) + x_left, :, y]
        from_right = all_kv.at[first(i) + x_right, :, y]
        await_bytes(from_left, x4_recv.at[0, i])
        await_bytes(from_right, x4_recv.at[1, i])
        if i % 2 == 0:
            send(from_left, from_left, x_send.at[1], x4_recv.at[2, i], right)
        else:
            send(from_right, from_right, x_send.at[1], x4_recv.at[2, i], left)

    def own_along_y4(i):
        await_bytes(all_kv.at[first(i) + x_far, :, y], x4_recv.at[2, i])
        mine = all_kv.at[pl.ds(first(i), NX), :, y]
        send(mine, mine, y_send.at[0], y4_recv.at[0, i], up)
        send(mine, mine, y_send.at[0], y4_recv.at[1, i], down)

    def far_along_y4(i):
        from_down = all_kv.at[pl.ds(first(i), NX), :, y_down]
        from_up = all_kv.at[pl.ds(first(i), NX), :, y_up]
        await_bytes(from_down, y4_recv.at[0, i])
        await_bytes(from_up, y4_recv.at[1, i])
        if i % 2 == 0:
            send(from_down, from_down, y_send.at[0], y4_recv.at[2, i], up)
        else:
            send(from_up, from_up, y_send.at[0], y4_recv.at[2, i], down)

    def to_mate4(i):
        await_bytes(all_kv.at[pl.ds(first(i), NX), :, y_far], y4_recv.at[2, i])
        whole = all_kv.at[pl.ds(first(i), NX)]
        send(whole, whole, mate_send.at[1], mate_recv.at[1], mate)

    row_stages = ((3, to_mate), (2, far_along_x), (0, own_along_x))
    all_stages = ((6, to_mate4), (5, far_along_y4), (3, own_along_y4), (2, far_along_x4), (0, own_along_x4))

    def run(stages, step):
        for lag, stage in stages:
            if 0 <= step - lag < NZ:
                stage(step - lag)

    row_steps = NZ + 3
    for step in range(row_steps):
        run(all_stages, step)
        run(row_stages, step)

    loads[5].wait()
    loads[6].wait()
    await_bytes(queries, q_recv.at[0])
    await_bytes(row_kv.at[pl.ds((1 - c) * NZ * NX, NZ * NX)], mate_recv.at[0])

    columns = out_ref.at[:, pl.ds(pl.multiple_of((SLICE * z + y) * HD, HD), HD)]
    columns4 = out_ref.at[:, pl.ds(pl.multiple_of((SLICE * z + NY) * HD, HD), HD)]

    def row_unit(u, _):
        for t in range(NZ + 6 - row_steps):
            @pl.when(u == 2 * t + 1)
            def _(t=t):
                run(all_stages, row_steps + t)

        k, a = lax.div(u, 2), lax.rem(u, 2)
        odd = lax.rem(k, 2)
        zd = lax.rem(z + NY + lax.div(k + odd, 2) * (2 * odd - 1), NZ)
        row = ((lax.div(zd, 2) * NX + x) * 2 + c) * 4 + lax.rem(zd, 2) * 2 + a
        mine = zd * 2 + a
        q_tile = queries[pl.ds(2 * mine, 2)].reshape(TILE, HD)
        attend_unit(row_kv, q_tile, results, mine, lists, row, lengths[row], scores)
        for half in range(2):
            yd = 2 * a + half
            src = results.at[mine, half]

            @pl.when((zd == z) & (yd == y))
            def _(src=src):
                pltpu.make_async_copy(src, columns, out_recv.at[0]).start()

            @pl.when((zd != z) | (yd != y))
            def _(src=src, yd=yd):
                send(src, columns, out_send.at[0], out_recv.at[0], device(x, yd, zd, c))
        return 0

    lax.fori_loop(0, NZ * 2, row_unit, 0)
    await_bytes(all_kv.at[pl.ds((1 - c) * NZ * NX, NZ * NX)], mate_recv.at[1])

    def all_unit(v, _):
        row = ((y * NX + x) * 2 + c) * 4 + v
        mine = NZ * 2 + v
        q_tile = queries[pl.ds(2 * mine, 2)].reshape(TILE, HD)
        attend_unit(all_kv, q_tile, results, mine, lists, row, lengths[row], scores)
        zd = 2 * y + lax.div(v, 2)
        for half in range(2):
            yd = 2 * lax.rem(v, 2) + half
            src = results.at[mine, half]

            @pl.when((zd == z) & (yd == y))
            def _(src=src):
                pltpu.make_async_copy(src, columns4, out_recv.at[0]).start()

            @pl.when((zd != z) | (yd != y))
            def _(src=src, yd=yd):
                send(src, columns4, out_send.at[1], out_recv.at[0], device(x, yd, zd, c))
        return 0

    lax.fori_loop(0, NY, all_unit, 0)

    await_bytes(pack_kv.at[pl.ds(0, NZ * NY - 1 + NZ - 1)], z_send.at[0])
    await_bytes(pack_q.at[pl.ds(0, NZ * NY - 1 + NZ - 1)], q_send.at[0])

    @pl.when(z_hi != y)
    def _():
        await_bytes(pack_q.at[0], q_send.at[1])
        await_bytes(pack_q.at[pl.ds(0, 2 * NY)], out_send.at[1])

    @pl.when(z_hi == y)
    def _():
        await_bytes(pack_q.at[pl.ds(0, 2 * NY - 1)], out_send.at[1])

    await_bytes(row_kv.at[pl.ds(0, 3 * NZ)], x_send.at[0])
    await_bytes(all_kv.at[pl.ds(0, 3 * NZ), :, 0], x_send.at[1])
    await_bytes(all_kv.at[pl.ds(0, 3 * NZ)], y_send.at[0])
    await_bytes(row_kv.at[pl.ds(0, NX * NZ)], mate_send.at[0])
    await_bytes(all_kv.at[pl.ds(0, NX * NZ)], mate_send.at[1])
    await_bytes(pack_q.at[pl.ds(0, NZ * NY - 1)], out_send.at[0])
    await_bytes(out_ref, out_recv.at[0])


def local(query, key_in, value, query_gain, key_gain, tile_lists, list_lengths):
    rows, width = query.shape
    listed = tile_lists.T
    bf16 = jnp.bfloat16
    hbm = pl.BlockSpec(memory_space=pl.ANY)
    dma = pltpu.SemaphoreType.DMA
    return pl.pallas_call(
        fused_kernel,
        out_shape=jax.ShapeDtypeStruct((rows, width), bf16),
        in_specs=[hbm] * 7,
        out_specs=hbm,
        scratch_shapes=[
            pltpu.VMEM((rows, width), bf16),
            pltpu.VMEM((rows, width), bf16),
            pltpu.VMEM((rows, width), bf16),
            pltpu.VMEM((1, width), jnp.float32),
            pltpu.VMEM((1, width), jnp.float32),
            pltpu.SMEM(listed.shape, jnp.int32),
            pltpu.SMEM(list_lengths.shape, jnp.int32),
            pltpu.VMEM((HEADS, 2, HALF, HD), bf16),
            pltpu.VMEM((HEADS, HALF, HD), bf16),
            pltpu.VMEM((BLOCKS, 2, NY, HALF, HD), bf16),
            pltpu.VMEM((BLOCKS, 2, NY, HALF, HD), bf16),
            pltpu.VMEM((2 * UNITS, HALF, HD), bf16),
            pltpu.VMEM((LIST, TILE, TILE), jnp.float32),
            pltpu.VMEM((UNITS, 2, HALF, HD), bf16),
            dma((7,)), dma((1,)), dma((2,)), dma((1,)), dma((2,)), dma((2,)), dma((2,)),
            dma((NZ,)), dma((NZ,)), dma((3, NZ)), dma((3, NZ)), dma((3, NZ)), dma((2,)), dma((1,)), dma((1,)),
        ],
        compiler_params=pltpu.CompilerParams(
            collective_id=0, has_side_effects=True, vmem_limit_bytes=56 * 2**20
        ),
        name="fused",
    )(
        query, key_in, value, query_gain.reshape(1, -1), key_gain.reshape(1, -1),
        listed, list_lengths,
    )


def solution(mesh):
    in_specs = (
        P(("seq", "head"), None),
        P(("seq", "head"), None),
        P(("seq", "head"), None),
        P(),
        P(),
        P(),
        P(),
    )
    out_specs = P(("seq", "head"), None)
    return jax.shard_map(local, mesh=mesh, in_specs=in_specs, out_specs=out_specs, check_vma=False)
```

time: 154 us -> 103 us (0.67); the launches traced: 152 us -> 103 us
  Pallas kernels: 145 us -> 101 us
  local copies, waits for them, and re-layouts: 6.91 us -> 1.97 us
    pallas_call x3 -> x1, Pallas kernels: 145 us -> 101 us  [local(): pl.pallas_call(fused_kernel, out_shape=jax.ShapeDtypeStruct((rows, width)...]
    unnamed x15 -> x1, local copies, waits for them, and re-layouts: 6.91 us -> 1.97 us
where the time goes in v2:
time: 103 us
  Pallas kernels  101 us (98%)
  local copies, waits for them, and re-layouts  1.97 us (2%)
    pallas_call x1, Pallas kernels, local(): pl.pallas_call(fused_kernel, out_shape=jax.ShapeDtypeStruct((rows, width)...  101 us

profile of v2, /device:TPU:56, one launch (start us, length us, event | category | flops | bytes accessed | tf_op | source)
XLA Modules:
  0.0 102.6 jit_solution(17636518324564096196)
XLA Ops:
  0.0 100.6 %fused.1 = bf16[64,5120]{1,0:T(8,128)(2,1)} custom-call(bf16[64,5120]{1,0:T(8,128)(2,1)} %q_hbm.1, bf16[64,5120]{1,0:T(8,128)(2,1)} %k_hbm.1, bf16[64,5120]{1,0:T(8,128)(2,1)} %v_hbm.1, f32[1,5120]{1,0:T(1,128)} %bitcast.3, f32[1,5120]{1,0:T(1,128)} %bitcast.4, s32[20,128]{1,0:T(8,128)} %bitcast.5, s32[128]{0:T(128)} %lengths_hbm.1), custom_call_target="tpu_custom_call" | custom-call | tf_op jit(solution)/shard_map/fused/pallas_call | solution.py:367
  100.6 2.0 %copy.9 = bf16[64,5120]{1,0:T(8,128)(2,1)} copy(bf16[64,5120]{1,0:T(8,128)(2,1)} %fused.1) | data formatting | bytes 1310720

commit v3 on v2

--- a/solution.py
+++ b/solution.py
@@ -20,6 +20,9 @@
 UNITS = 20
 BLOCKS = NC * NZ * NX
 MESH = pl.DeviceIdType.MESH
+COMBINE_AT = 8
+ROW_DELAY = 4
+PART_UNITS = {12: 4, 13: 3, 14: 3, 15: 3, 16: 3}
 OFFSETS = (0, 1, 7, 2, 6, 3, 5, 4)
 
 
@@ -111,12 +114,52 @@
     out_ref[out_index] = (acc / summed).astype(jnp.bfloat16).reshape(2, HALF, HD)
 
 
+def attend_part(kv, q_tile, out_ref, stats, u, lists, row, length, mine, scores):
+    lane = lax.broadcasted_iota(jnp.int32, (TILE, HD), 1)
+    at = []
+    bias = []
+    for n in range(LIST):
+        entry = lists[n, row]
+        z = ((entry >> 5) << 1) + ((entry >> 1) & 1)
+        at.append((((entry >> 2) & 1) * NZ + z) * NX + ((entry >> 3) & 3))
+        bias.append(jnp.where((n < length) & ((entry & 1) == mine), 0.0, -1e30))
+    high = None
+    for n in range(0, LIST, 2 * PAIR):
+        keys = jnp.concatenate([kv[at[m], 0] for m in range(n, n + 2 * PAIR)], axis=0)
+        both = lax.dot_general(
+            q_tile, keys, (((1,), (1,)), ((), ())), preferred_element_type=jnp.float32
+        )
+        for m in range(n, n + 2 * PAIR, 2):
+            s = both[:, (m - n) * HALF:(m - n + 2) * HALF]
+            s = s + jnp.where(lane[:1] < HALF, bias[m], bias[m + 1])
+            scores[m // 2] = s
+            high = s if high is None else jnp.maximum(high, s)
+    row_high = jnp.max(high, axis=1, keepdims=True)
+    total = None
+    acc = None
+    for n in range(0, LIST, 2 * PAIR):
+        weights = []
+        for m in range(n, n + 2 * PAIR, 2):
+            raw = jnp.exp2((scores[m // 2] - row_high) * LOG2_SCALE)
+            total = raw if total is None else total + raw
+            weights.append(raw.astype(jnp.bfloat16))
+        values = jnp.concatenate([kv[at[m], 1] for m in range(n, n + 2 * PAIR)], axis=0)
+        mixed = jnp.dot(
+            jnp.concatenate(weights, axis=1), values, preferred_element_type=jnp.float32
+        )
+        acc = mixed if acc is None else acc + mixed
+    summed = jnp.sum(total, axis=1, keepdims=True)
+    out_ref[u] = (acc / summed).astype(jnp.bfloat16)
+    log_sum = row_high * LOG2_SCALE + jnp.log(summed) * math.log2(math.e)
+    stats[...] = jnp.where(lane == u, log_sum, stats[...])
+
+
 def fused_kernel(
     q_hbm, k_hbm, v_hbm, qg_hbm, kg_hbm, lists_hbm, lengths_hbm, out_ref,
     q_ref, k_ref, v_ref, qg_ref, kg_ref, lists, lengths,
-    pack_kv, pack_q, row_kv, all_kv, queries, scores, results,
-    load_sem, z_send, x_send, y_send, mate_send, q_send, out_send,
-    zr_recv, z4_recv, xr_recv, x4_recv, y4_recv, mate_recv, q_recv, out_recv,
+    pack_kv, pack_q, row_kv, all_kv, queries, queries4, scores, results, parts_out, parts, stats, all_stats,
+    load_sem, z_send, x_send, mate_send, q_send, out_send, part_send,
+    zr_recv, z4_recv, xr_recv, x4_recv, mate_recv, q_recv, q4_recv, part_recv, out_recv,
 ):
     loads = []
     for n, (src, dst) in enumerate((
@@ -135,8 +178,6 @@
                 partners.append(device(x, lax.rem(y + dy, NY), lax.rem(z + dz, NZ), c))
     right = device(lax.rem(x + 1, NX), y, z, c)
     left = device(lax.rem(x + NX - 1, NX), y, z, c)
-    up = device(x, lax.rem(y + 1, NY), z, c)
-    down = device(x, lax.rem(y + NY - 1, NY), z, c)
     mate = device(x, y, z, 1 - c)
     partners += [right, left, mate]
     for target in partners:
@@ -158,6 +199,14 @@
     pl.semaphore_wait(barrier, len(partners))
 
     block = (c * NZ + z) * NX + x
+    for i, dz in enumerate(OFFSETS):
+        zd = lax.rem(z + dz, NZ)
+        src = pack_kv.at[SLICE * zd + NY]
+        dst = all_kv.at[block]
+        if dz:
+            send(src, dst, z_send.at[0], z4_recv.at[i], device(x, y, zd, c))
+        else:
+            pltpu.make_async_copy(src, dst, z4_recv.at[i]).start()
     for i, dz in enumerate(OFFSETS):
         zd = lax.rem(z + dz, NZ)
         for dy in range(NY):
@@ -168,18 +217,19 @@
                 send(src, dst, z_send.at[0], zr_recv.at[i], device(x, yd, zd, c))
             else:
                 pltpu.make_async_copy(src, dst, zr_recv.at[i]).start()
-        src = pack_kv.at[SLICE * zd + NY]
-        dst = all_kv.at[block, :, y]
-        if dz:
-            send(src, dst, z_send.at[0], z4_recv.at[i], device(x, y, zd, c))
-        else:
-            pltpu.make_async_copy(src, dst, z4_recv.at[i]).start()
 
     loads[3].wait()
     loads[4].wait()
     normalize_into(q_ref, qg_ref, put_q)
-    z_hi, z_lo = lax.div(z, 2), lax.rem(z, 2)
-    for i, dz in enumerate(OFFSETS):
+    for dz in OFFSETS:
+        zd = lax.rem(z + dz, NZ)
+        src = pack_q.at[SLICE * zd + NY]
+        dst = queries4.at[z, y]
+        if dz:
+            send(src, dst, q_send.at[0], q4_recv.at[0], device(x, y, zd, c))
+        else:
+            pltpu.make_async_copy(src, dst, q4_recv.at[0]).start()
+    for dz in OFFSETS:
         zd = lax.rem(z + dz, NZ)
         for dy in range(NY):
             yd = lax.rem(y + dy, NY)
@@ -189,21 +239,8 @@
                 send(src, dst, q_send.at[0], q_recv.at[0], device(x, yd, zd, c))
             else:
                 pltpu.make_async_copy(src, dst, q_recv.at[0]).start()
-        src = pack_q.at[SLICE * zd + NY]
-        dst = queries.at[NZ * NY + z_lo * NY + y]
-        if dz:
-            send(src, dst, q_send.at[0], q_recv.at[0], device(x, z_hi, zd, c))
-        else:
-            @pl.when(z_hi == y)
-            def _(src=src, dst=dst):
-                pltpu.make_async_copy(src, dst, q_recv.at[0]).start()
-
-            @pl.when(z_hi != y)
-            def _(src=src, dst=dst, zd=zd):
-                send(src, dst, q_send.at[1], q_recv.at[0], device(x, z_hi, zd, c))
 
     x_left, x_right, x_far = lax.rem(x + NX - 1, NX), lax.rem(x + 1, NX), lax.rem(x + 2, NX)
-    y_down, y_up, y_far = lax.rem(y + NY - 1, NY), lax.rem(y + 1, NY), lax.rem(y + 2, NY)
 
     def first(i):
         return (c * NZ + lax.rem(z + NZ - OFFSETS[i], NZ)) * NX
@@ -219,10 +256,10 @@
         from_right = row_kv.at[first(i) + x_right]
         await_bytes(from_left, xr_recv.at[0, i])
         await_bytes(from_right, xr_recv.at[1, i])
-        if i % 2 == 0:
-            send(from_left, from_left, x_send.at[0], xr_recv.at[2, i], right)
-        else:
-            send(from_right, from_right, x_send.at[0], xr_recv.at[2, i], left)
+        from_left = row_kv.at[first(i) + x_left, 0]
+        from_right = row_kv.at[first(i) + x_right, 1]
+        send(from_left, from_left, x_send.at[0], xr_recv.at[2, i], right)
+        send(from_right, from_right, x_send.at[0], xr_recv.at[2, i], left)
 
     def to_mate(i):
         await_bytes(row_kv.at[first(i) + x_far], xr_recv.at[2, i])
@@ -230,68 +267,128 @@
         send(whole, whole, mate_send.at[0], mate_recv.at[0], mate)
 
     def own_along_x4(i):
-        mine = all_kv.at[first(i) + x, :, y]
+        mine = all_kv.at[first(i) + x]
         await_bytes(mine, z4_recv.at[i])
         send(mine, mine, x_send.at[1], x4_recv.at[0, i], right)
         send(mine, mine, x_send.at[1], x4_recv.at[1, i], left)
 
     def far_along_x4(i):
-        from_left = all_kv.at[first(i) + x_left, :, y]
-        from_right = all_kv.at[first(i) + x_right, :, y]
+        from_left = all_kv.at[first(i) + x_left]
+        from_right = all_kv.at[first(i) + x_right]
         await_bytes(from_left, x4_recv.at[0, i])
         await_bytes(from_right, x4_recv.at[1, i])
-        if i % 2 == 0:
-            send(from_left, from_left, x_send.at[1], x4_recv.at[2, i], right)
-        else:
-            send(from_right, from_right, x_send.at[1], x4_recv.at[2, i], left)
-
-    def own_along_y4(i):
-        await_bytes(all_kv.at[first(i) + x_far, :, y], x4_recv.at[2, i])
-        mine = all_kv.at[pl.ds(first(i), NX), :, y]
-        send(mine, mine, y_send.at[0], y4_recv.at[0, i], up)
-        send(mine, mine, y_send.at[0], y4_recv.at[1, i], down)
-
-    def far_along_y4(i):
-        from_down = all_kv.at[pl.ds(first(i), NX), :, y_down]
-        from_up = all_kv.at[pl.ds(first(i), NX), :, y_up]
-        await_bytes(from_down, y4_recv.at[0, i])
-        await_bytes(from_up, y4_recv.at[1, i])
-        if i % 2 == 0:
-            send(from_down, from_down, y_send.at[0], y4_recv.at[2, i], up)
-        else:
-            send(from_up, from_up, y_send.at[0], y4_recv.at[2, i], down)
+        from_left = all_kv.at[first(i) + x_left, 0]
+        from_right = all_kv.at[first(i) + x_right, 1]
+        send(from_left, from_left, x_send.at[1], x4_recv.at[2, i], right)
+        send(from_right, from_right, x_send.at[1], x4_recv.at[2, i], left)
 
     def to_mate4(i):
-        await_bytes(all_kv.at[pl.ds(first(i), NX), :, y_far], y4_recv.at[2, i])
+        await_bytes(all_kv.at[first(i) + x_far], x4_recv.at[2, i])
         whole = all_kv.at[pl.ds(first(i), NX)]
         send(whole, whole, mate_send.at[1], mate_recv.at[1], mate)
 
-    row_stages = ((3, to_mate), (2, far_along_x), (0, own_along_x))
-    all_stages = ((6, to_mate4), (5, far_along_y4), (3, own_along_y4), (2, far_along_x4), (0, own_along_x4))
+    def spread_queries4():
+        mine = queries4.at[:, y]
+        await_bytes(mine, q4_recv.at[0])
+        for dy in range(1, NY):
+            target = device(x, lax.rem(y + dy, NY), z, c)
+            send(mine, mine, q_send.at[1], q4_recv.at[dy], target)
+
+    def gather_fifth():
+        loads[5].wait()
+        loads[6].wait()
+        for dy in range(1, NY):
+            await_bytes(queries4.at[:, lax.rem(y + NY - dy, NY)], q4_recv.at[dy])
+        await_bytes(all_kv.at[pl.ds((1 - c) * NZ * NX, NZ * NX)], mate_recv.at[1])
+
+    def part_unit(n, _):
+        group = lax.rem(y + 1 + lax.div(n, NY), NY)
+        v = lax.rem(n, NY)
+        u = group * NY + v
+        row = ((group * NX + x) * 2 + c) * 4 + v
+        q_tile = queries4[lax.div(u, 2), pl.ds(2 * lax.rem(u, 2), 2)].reshape(TILE, HD)
+        attend_part(all_kv, q_tile, parts_out, stats, u, lists, row, lengths[row], lax.div(y, 2), scores)
+        src = parts_out.at[u]
+        dst = parts.at[y, v]
+
+        @pl.when(group == y)
+        def _():
+            pltpu.make_async_copy(src, dst, part_recv.at[0]).start()
+
+        @pl.when(group != y)
+        def _():
+            send(src, dst, part_send.at[0], part_recv.at[0], device(x, group, z, c))
+        return 0
+
+    row_stages = ((5, to_mate), (3, far_along_x), (0, own_along_x))
+    all_stages = ((4, to_mate4), (2, far_along_x4), (0, own_along_x4))
 
     def run(stages, step):
         for lag, stage in stages:
             if 0 <= step - lag < NZ:
                 stage(step - lag)
 
-    row_steps = NZ + 3
-    for step in range(row_steps):
+    stats[...] = jnp.zeros_like(stats)
+    done = 0
+    for step in range(NZ + ROW_DELAY + 5):
         run(all_stages, step)
-        run(row_stages, step)
-
-    loads[5].wait()
-    loads[6].wait()
+        run(row_stages, step - ROW_DELAY)
+        if step == NZ:
+            spread_queries4()
+        count = PART_UNITS.get(step, 0)
+        if count:
+            if not done:
+                gather_fifth()
+            lax.fori_loop(done, done + count, part_unit, 0)
+            done += count
+    assert done == NZ * 2
+    for dy in range(NY):
+        dst = all_stats.at[y]
+        if dy:
+            target = device(x, lax.rem(y + dy, NY), z, c)
+            send(stats, dst, part_send.at[1], part_recv.at[1], target)
+        else:
+            pltpu.make_async_copy(stats, dst, part_recv.at[1]).start()
+
     await_bytes(queries, q_recv.at[0])
     await_bytes(row_kv.at[pl.ds((1 - c) * NZ * NX, NZ * NX)], mate_recv.at[0])
 
     columns = out_ref.at[:, pl.ds(pl.multiple_of((SLICE * z + y) * HD, HD), HD)]
     columns4 = out_ref.at[:, pl.ds(pl.multiple_of((SLICE * z + NY) * HD, HD), HD)]
 
+    def combine():
+        await_bytes(parts, part_recv.at[0])
+        await_bytes(all_stats, part_recv.at[1])
+        lane = lax.broadcasted_iota(jnp.int32, (TILE, HD), 1)
+        for v in range(NY):
+            sums = [
+                jnp.sum(jnp.where(lane == y * NY + v, all_stats[k], 0.0), axis=1, keepdims=True)
+                for k in range(NY)
+            ]
+            top = jnp.maximum(jnp.maximum(sums[0], sums[1]), jnp.maximum(sums[2], sums[3]))
+            shares = [jnp.exp2(part - top) for part in sums]
+            whole = shares[0] + shares[1] + shares[2] + shares[3]
+            mixed = shares[0] * parts[0, v].astype(jnp.float32)
+            for k in range(1, NY):
+                mixed = mixed + shares[k] * parts[k, v].astype(jnp.float32)
+            results[NZ * 2 + v] = (mixed / whole).astype(jnp.bfloat16).reshape(2, HALF, HD)
+            zd = 2 * y + v // 2
+            for half in range(2):
+                yd = 2 * (v % 2) + half
+                src = results.at[NZ * 2 + v, half]
+
+                @pl.when((zd == z) & (yd == y))
+                def _(src=src):
+                    pltpu.make_async_copy(src, columns4, out_recv.at[0]).start()
+
+                @pl.when((zd != z) | (yd != y))
+                def _(src=src, yd=yd, zd=zd):
+                    send(src, columns4, out_send.at[1], out_recv.at[0], device(x, yd, zd, c))
+
     def row_unit(u, _):
-        for t in range(NZ + 6 - row_steps):
-            @pl.when(u == 2 * t + 1)
-            def _(t=t):
-                run(all_stages, row_steps + t)
+        @pl.when(u == COMBINE_AT)
+        def _():
+            combine()
 
         k, a = lax.div(u, 2), lax.rem(u, 2)
         odd = lax.rem(k, 2)
@@ -314,44 +411,22 @@
         return 0
 
     lax.fori_loop(0, NZ * 2, row_unit, 0)
-    await_bytes(all_kv.at[pl.ds((1 - c) * NZ * NX, NZ * NX)], mate_recv.at[1])
-
-    def all_unit(v, _):
-        row = ((y * NX + x) * 2 + c) * 4 + v
-        mine = NZ * 2 + v
-        q_tile = queries[pl.ds(2 * mine, 2)].reshape(TILE, HD)
-        attend_unit(all_kv, q_tile, results, mine, lists, row, lengths[row], scores)
-        zd = 2 * y + lax.div(v, 2)
-        for half in range(2):
-            yd = 2 * lax.rem(v, 2) + half
-            src = results.at[mine, half]
-
-            @pl.when((zd == z) & (yd == y))
-            def _(src=src):
-                pltpu.make_async_copy(src, columns4, out_recv.at[0]).start()
-
-            @pl.when((zd != z) | (yd != y))
-            def _(src=src, yd=yd):
-                send(src, columns4, out_send.at[1], out_recv.at[0], device(x, yd, zd, c))
-        return 0
-
-    lax.fori_loop(0, NY, all_unit, 0)
-
     await_bytes(pack_kv.at[pl.ds(0, NZ * NY - 1 + NZ - 1)], z_send.at[0])
     await_bytes(pack_q.at[pl.ds(0, NZ * NY - 1 + NZ - 1)], q_send.at[0])
 
-    @pl.when(z_hi != y)
+    @pl.when(lax.div(z, 2) != y)
     def _():
-        await_bytes(pack_q.at[0], q_send.at[1])
         await_bytes(pack_q.at[pl.ds(0, 2 * NY)], out_send.at[1])
 
-    @pl.when(z_hi == y)
+    @pl.when(lax.div(z, 2) == y)
     def _():
         await_bytes(pack_q.at[pl.ds(0, 2 * NY - 1)], out_send.at[1])
 
+    await_bytes(pack_q.at[pl.ds(0, (NY - 1) * NZ)], q_send.at[1])
+    await_bytes(parts_out.at[pl.ds(0, (NY - 1) * NY)], part_send.at[0])
+    await_bytes(all_stats.at[pl.ds(0, NY - 1)], part_send.at[1])
     await_bytes(row_kv.at[pl.ds(0, 3 * NZ)], x_send.at[0])
-    await_bytes(all_kv.at[pl.ds(0, 3 * NZ), :, 0], x_send.at[1])
-    await_bytes(all_kv.at[pl.ds(0, 3 * NZ)], y_send.at[0])
+    await_bytes(all_kv.at[pl.ds(0, 3 * NZ)], x_send.at[1])
     await_bytes(row_kv.at[pl.ds(0, NX * NZ)], mate_send.at[0])
     await_bytes(all_kv.at[pl.ds(0, NX * NZ)], mate_send.at[1])
     await_bytes(pack_q.at[pl.ds(0, NZ * NY - 1)], out_send.at[0])
@@ -380,12 +455,17 @@
             pltpu.VMEM((HEADS, 2, HALF, HD), bf16),
             pltpu.VMEM((HEADS, HALF, HD), bf16),
             pltpu.VMEM((BLOCKS, 2, NY, HALF, HD), bf16),
-            pltpu.VMEM((BLOCKS, 2, NY, HALF, HD), bf16),
-            pltpu.VMEM((2 * UNITS, HALF, HD), bf16),
+            pltpu.VMEM((BLOCKS, 2, HALF, HD), bf16),
+            pltpu.VMEM((NZ * NY, HALF, HD), bf16),
+            pltpu.VMEM((NZ, NY, HALF, HD), bf16),
             pltpu.VMEM((LIST, TILE, TILE), jnp.float32),
             pltpu.VMEM((UNITS, 2, HALF, HD), bf16),
-            dma((7,)), dma((1,)), dma((2,)), dma((1,)), dma((2,)), dma((2,)), dma((2,)),
-            dma((NZ,)), dma((NZ,)), dma((3, NZ)), dma((3, NZ)), dma((3, NZ)), dma((2,)), dma((1,)), dma((1,)),
+            pltpu.VMEM((NZ * 2, TILE, HD), bf16),
+            pltpu.VMEM((NY, NY, TILE, HD), bf16),
+            pltpu.VMEM((TILE, HD), jnp.float32),
+            pltpu.VMEM((NY, TILE, HD), jnp.float32),
+            dma((7,)), dma((1,)), dma((2,)), dma((2,)), dma((2,)), dma((2,)), dma((2,)),
+            dma((NZ,)), dma((NZ,)), dma((3, NZ)), dma((3, NZ)), dma((2,)), dma((1,)), dma((NY,)), dma((2,)), dma((1,)),
         ],
         compiler_params=pltpu.CompilerParams(
             collective_id=0, has_side_effects=True, vmem_limit_bytes=56 * 2**20

time: 103 us -> 94.3 us (0.916); the launches traced: 103 us -> 92.5 us
  Pallas kernels: 101 us -> 90.5 us
    pallas_call x1, Pallas kernels: 101 us -> 90.5 us  [local(): pl.pallas_call(fused_kernel, out_shape=jax.ShapeDtypeStruct((rows, width)...]
where the time goes in v3:
time: 94.3 us; the launch traced here: 92.5 us
  Pallas kernels  90.5 us (96%)
  local copies, waits for them, and re-layouts  1.97 us (2%)
    pallas_call x1, Pallas kernels, local(): pl.pallas_call(fused_kernel, out_shape=jax.ShapeDtypeStruct((rows, width)...  90.5 us
    unnamed x1, local copies, waits for them, and re-layouts  1.97 us

profile of v3, /device:TPU:56, one launch (start us, length us, event | category | flops | bytes accessed | tf_op | source)
XLA Modules:
  0.0 92.5 jit_solution(10247331199594981110)
XLA Ops:
  0.0 90.5 %fused.1 = bf16[64,5120]{1,0:T(8,128)(2,1)} custom-call(bf16[64,5120]{1,0:T(8,128)(2,1)} %q_hbm.1, bf16[64,5120]{1,0:T(8,128)(2,1)} %k_hbm.1, bf16[64,5120]{1,0:T(8,128)(2,1)} %v_hbm.1, f32[1,5120]{1,0:T(1,128)} %bitcast.3, f32[1,5120]{1,0:T(1,128)} %bitcast.4, s32[20,128]{1,0:T(8,128)} %bitcast.5, s32[128]{0:T(128)} %lengths_hbm.1), custom_call_target="tpu_custom_call" | custom-call | tf_op jit(solution)/shard_map/fused/pallas_call | solution.py:442
  90.6 2.0 %copy.9 = bf16[64,5120]{1,0:T(8,128)(2,1)} copy(bf16[64,5120]{1,0:T(8,128)(2,1)} %fused.1) | data formatting | bytes 1310720

commit v4 on v3

--- a/solution.py
+++ b/solution.py
@@ -20,9 +20,11 @@
 UNITS = 20
 BLOCKS = NC * NZ * NX
 MESH = pl.DeviceIdType.MESH
-COMBINE_AT = 8
-ROW_DELAY = 4
-PART_UNITS = {12: 4, 13: 3, 14: 3, 15: 3, 16: 3}
+COMBINE_AT = 15
+ROW_DELAY = 2
+PART_UNITS = {11: 3, 12: 3, 13: 3, 14: 3, 15: 2, 16: 2}
+QUERY_STEPS = (5, 5, 6, 6, 7, 7, 8, 8)
+KV_STEPS = (-1, -1, -1, -1, -1, -1, -1, -1)
 OFFSETS = (0, 1, 7, 2, 6, 3, 5, 4)
 
 
@@ -157,7 +159,7 @@
 def fused_kernel(
     q_hbm, k_hbm, v_hbm, qg_hbm, kg_hbm, lists_hbm, lengths_hbm, out_ref,
     q_ref, k_ref, v_ref, qg_ref, kg_ref, lists, lengths,
-    pack_kv, pack_q, row_kv, all_kv, queries, queries4, scores, results, parts_out, parts, stats, all_stats,
+    pack_kv, pack_q, row_kv, all_kv, queries, queries4, scores, results, parts_out, parts, stats, all_stats, landing,
     load_sem, z_send, x_send, mate_send, q_send, out_send, part_send,
     zr_recv, z4_recv, xr_recv, x4_recv, mate_recv, q_recv, q4_recv, part_recv, out_recv,
 ):
@@ -207,7 +209,8 @@
             send(src, dst, z_send.at[0], z4_recv.at[i], device(x, y, zd, c))
         else:
             pltpu.make_async_copy(src, dst, z4_recv.at[i]).start()
-    for i, dz in enumerate(OFFSETS):
+    def issue_row_kv(i):
+        dz = OFFSETS[i]
         zd = lax.rem(z + dz, NZ)
         for dy in range(NY):
             yd = lax.rem(y + dy, NY)
@@ -217,6 +220,10 @@
                 send(src, dst, z_send.at[0], zr_recv.at[i], device(x, yd, zd, c))
             else:
                 pltpu.make_async_copy(src, dst, zr_recv.at[i]).start()
+
+    for i in range(NZ):
+        if KV_STEPS[i] < 0:
+            issue_row_kv(i)
 
     loads[3].wait()
     loads[4].wait()
@@ -229,7 +236,7 @@
             send(src, dst, q_send.at[0], q4_recv.at[0], device(x, y, zd, c))
         else:
             pltpu.make_async_copy(src, dst, q4_recv.at[0]).start()
-    for dz in OFFSETS:
+    def issue_queries(dz):
         zd = lax.rem(z + dz, NZ)
         for dy in range(NY):
             yd = lax.rem(y + dy, NY)
@@ -320,7 +327,7 @@
             send(src, dst, part_send.at[0], part_recv.at[0], device(x, group, z, c))
         return 0
 
-    row_stages = ((5, to_mate), (3, far_along_x), (0, own_along_x))
+    row_stages = ((7, to_mate), (4, far_along_x), (0, own_along_x))
     all_stages = ((4, to_mate4), (2, far_along_x4), (0, own_along_x4))
 
     def run(stages, step):
@@ -330,9 +337,14 @@
 
     stats[...] = jnp.zeros_like(stats)
     done = 0
-    for step in range(NZ + ROW_DELAY + 5):
+    for step in range(NZ + ROW_DELAY + 7):
         run(all_stages, step)
         run(row_stages, step - ROW_DELAY)
+        for i, dz in enumerate(OFFSETS):
+            if QUERY_STEPS[i] == step:
+                issue_queries(dz)
+            if KV_STEPS[i] == step:
+                issue_row_kv(i)
         if step == NZ:
             spread_queries4()
         count = PART_UNITS.get(step, 0)
@@ -353,8 +365,8 @@
     await_bytes(queries, q_recv.at[0])
     await_bytes(row_kv.at[pl.ds((1 - c) * NZ * NX, NZ * NX)], mate_recv.at[0])
 
-    columns = out_ref.at[:, pl.ds(pl.multiple_of((SLICE * z + y) * HD, HD), HD)]
-    columns4 = out_ref.at[:, pl.ds(pl.multiple_of((SLICE * z + NY) * HD, HD), HD)]
+    columns = landing.at[SLICE * z + y]
+    columns4 = landing.at[SLICE * z + NY]
 
     def combine():
         await_bytes(parts, part_recv.at[0])
@@ -430,7 +442,9 @@
     await_bytes(row_kv.at[pl.ds(0, NX * NZ)], mate_send.at[0])
     await_bytes(all_kv.at[pl.ds(0, NX * NZ)], mate_send.at[1])
     await_bytes(pack_q.at[pl.ds(0, NZ * NY - 1)], out_send.at[0])
-    await_bytes(out_ref, out_recv.at[0])
+    await_bytes(landing, out_recv.at[0])
+    for h in range(HEADS):
+        out_ref[:, h * HD:(h + 1) * HD] = landing[h]
 
 
 def local(query, key_in, value, query_gain, key_gain, tile_lists, list_lengths):
@@ -443,7 +457,7 @@
         fused_kernel,
         out_shape=jax.ShapeDtypeStruct((rows, width), bf16),
         in_specs=[hbm] * 7,
-        out_specs=hbm,
+        out_specs=pl.BlockSpec(memory_space=pltpu.VMEM),
         scratch_shapes=[
             pltpu.VMEM((rows, width), bf16),
             pltpu.VMEM((rows, width), bf16),
@@ -464,6 +478,7 @@
             pltpu.VMEM((NY, NY, TILE, HD), bf16),
             pltpu.VMEM((TILE, HD), jnp.float32),
             pltpu.VMEM((NY, TILE, HD), jnp.float32),
+            pltpu.VMEM((HEADS, HALF, HD), bf16),
             dma((7,)), dma((1,)), dma((2,)), dma((2,)), dma((2,)), dma((2,)), dma((2,)),
             dma((NZ,)), dma((NZ,)), dma((3, NZ)), dma((3, NZ)), dma((2,)), dma((1,)), dma((NY,)), dma((2,)), dma((1,)),
         ],

time: 94.3 us -> 92.2 us (0.978); the launches traced: 92.5 us -> 92.1 us
  no operation moved by 1% of the time
where the time goes in v4:
time: 92.2 us; the launch traced here: 92.1 us
  Pallas kernels  90.1 us (98%)
  local copies, waits for them, and re-layouts  1.97 us (2%)
    pallas_call x1, Pallas kernels, local(): pl.pallas_call(fused_kernel, out_shape=jax.ShapeDtypeStruct((rows, width)...  90.1 us
    unnamed x1, local copies, waits for them, and re-layouts  1.97 us

profile of v4, /device:TPU:56, one launch (start us, length us, event | category | flops | bytes accessed | tf_op | source)
XLA Modules:
  0.0 92.1 jit_solution(6561687522624488004)
XLA Ops:
  0.0 90.1 %fused.1 = bf16[64,5120]{1,0:T(8,128)(2,1)} custom-call(bf16[64,5120]{1,0:T(8,128)(2,1)} %q_hbm.1, bf16[64,5120]{1,0:T(8,128)(2,1)} %k_hbm.1, bf16[64,5120]{1,0:T(8,128)(2,1)} %v_hbm.1, f32[1,5120]{1,0:T(1,128)} %bitcast.3, f32[1,5120]{1,0:T(1,128)} %bitcast.4, s32[20,128]{1,0:T(8,128)} %bitcast.5, s32[128]{0:T(128)} %lengths_hbm.1), custom_call_target="tpu_custom_call" | custom-call | tf_op jit(solution)/shard_map/fused/pallas_call | solution.py:456
  90.1 2.0 %copy.9 = bf16[64,5120]{1,0:T(8,128)(2,1)} copy(bf16[64,5120]{1,0:T(8,128)(2,1)} %fused.1) | data formatting | bytes 1310720

commit v5 on v4

--- a/solution.py
+++ b/solution.py
@@ -22,10 +22,10 @@
 MESH = pl.DeviceIdType.MESH
 COMBINE_AT = 15
 ROW_DELAY = 2
-PART_UNITS = {11: 3, 12: 3, 13: 3, 14: 3, 15: 2, 16: 2}
+PART_UNITS = {11: 2, 12: 2, 13: 2, 14: 2, 15: 4, 16: 4}
 QUERY_STEPS = (5, 5, 6, 6, 7, 7, 8, 8)
 KV_STEPS = (-1, -1, -1, -1, -1, -1, -1, -1)
-OFFSETS = (0, 1, 7, 2, 6, 3, 5, 4)
+OFFSETS = (0, 1, 7, 2, 6, 4, 3, 5)
 
 
 def place():

time: 92.2 us -> 91.6 us (level)
  no operation moved by 1% of the time
where the time goes in v5:
time: 91.6 us; the launch traced here: 91.5 us
  Pallas kernels  89.5 us (98%)
  local copies, waits for them, and re-layouts  1.97 us (2%)
    pallas_call x1, Pallas kernels, local(): pl.pallas_call(fused_kernel, out_shape=jax.ShapeDtypeStruct((rows, width)...  89.5 us
    unnamed x1, local copies, waits for them, and re-layouts  1.97 us

profile of v5, /device:TPU:56, one launch (start us, length us, event | category | flops | bytes accessed | tf_op | source)
XLA Modules:
  0.0 91.5 jit_solution(2922377163358145601)
XLA Ops:
  0.0 89.5 %fused.1 = bf16[64,5120]{1,0:T(8,128)(2,1)} custom-call(bf16[64,5120]{1,0:T(8,128)(2,1)} %q_hbm.1, bf16[64,5120]{1,0:T(8,128)(2,1)} %k_hbm.1, bf16[64,5120]{1,0:T(8,128)(2,1)} %v_hbm.1, f32[1,5120]{1,0:T(1,128)} %bitcast.3, f32[1,5120]{1,0:T(1,128)} %bitcast.4, s32[20,128]{1,0:T(8,128)} %bitcast.5, s32[128]{0:T(128)} %lengths_hbm.1), custom_call_target="tpu_custom_call" | custom-call | tf_op jit(solution)/shard_map/fused/pallas_call | solution.py:456
  89.5 2.0 %copy.9 = bf16[64,5120]{1,0:T(8,128)(2,1)} copy(bf16[64,5120]{1,0:T(8,128)(2,1)} %fused.1) | data formatting | bytes 1310720
